TPU v7x, 256 devices: a whole 4x4x8 slice. The times are simulated.
256 devices in a mesh: tm: 128 (over x, z, y_hi, core), mp: 2 (over y_lo).
Axes of the slice: x: 4, y: 4 (y_hi: 2, y_lo: 2; y = y_hi * 2 + y_lo), z: 8, core: 2. Of those that a mesh axis runs over, the one named last changes fastest.
Arguments:
- patches: bfloat16 [20480, 768], P('tm'), may hold values from -6 to 6
- keep_mask: int32 [20480], replicated, may hold values from 0 to 1, as said below
- segment: int32 [20480], replicated, may hold values from 0 to 255, never falling along the last dimension, each value on 1 to 160 neighbouring positions
- w_query: bfloat16 [768, 768], P(None, 'mp'), may hold values from -0.4375 to 0.4375
- w_key: bfloat16 [768, 768], P(None, 'mp'), may hold values from -0.4375 to 0.4375
- w_value: bfloat16 [768, 768], P(None, 'mp'), may hold values from -0.21875 to 0.21875
- w_out: bfloat16 [768, 768], P('mp'), may hold values from -0.4375 to 0.4375
- w_cross_query: bfloat16 [768, 768], P(None, 'mp'), may hold values from -0.375 to 0.375
- w_cross_out: bfloat16 [768, 768], P('mp'), may hold values from -0.21875 to 0.21875
- w_up: bfloat16 [768, 3072], P(None, 'mp'), may hold values from -0.21875 to 0.21875
- w_down: bfloat16 [3072, 768], P('mp'), may hold values from -0.109375 to 0.109375
Outputs:
- updated: bfloat16 [20480, 768], P('tm')
Inputs may be any that keep to these rules, and one draw needn't show every extreme that they name: `keep_mask`: each run of 160 patches from the start (one index of tm) keeps between 24 and 72 patches, 6144 in all; the kept patches before the j-th run number j * 48 plus at most 12 and minus at most 12, with a difference of exactly 12 in some run; some run keeps exactly 72. Segment numbers never fall along the patches; each segment covers 1 to 160 patches, one exactly 160.
All inputs are finite; a program needn't handle non-finite values.
Results may differ from a plain program's by a relative error of at most 0.0081.
Values may be sent and summed in bfloat16 or wider, within the bound.
A program may use at most 128 MiB of HBM per device.

v0:
```python
import jax
import jax.numpy as jnp
from jax import lax
from jax.sharding import PartitionSpec as P

HD = 64
MOST_KEEP = 72


def with_halo(block, sides, width):
    for axis, dim in sides:
        count = lax.axis_size(axis)
        forward = [(i, i + 1) for i in range(count - 1)]
        backward = [(target, source) for source, target in forward]
        low = lax.ppermute(
            lax.slice_in_dim(block, block.shape[dim] - width, None, axis=dim), axis, forward
        )
        high = lax.ppermute(lax.slice_in_dim(block, 0, width, axis=dim), axis, backward)
        block = jnp.concatenate([low, block, high], axis=dim)
    return block


def norm_rows(values):
    values = values.astype(jnp.float32)
    center = values - jnp.mean(values, axis=-1, keepdims=True)
    return center * lax.rsqrt(jnp.mean(center * center, axis=-1, keepdims=True) + 1e-05)


def split_heads(values):
    return values.reshape(values.shape[0], values.shape[1] // HD, HD)


def attend_block(running, queries, key_rows, value_rows, usable):
    numerator, denominator = running
    scores = jnp.einsum(
        "rhe,mhe->rhm", queries, key_rows, preferred_element_type=jnp.float32
    ) * HD ** (-0.5)
    weight = jnp.where(usable[:, None, :], jnp.exp(scores), 0.0)
    numerator = numerator + jnp.einsum(
        "rhm,mhe->rhe", weight.astype(jnp.bfloat16), value_rows, preferred_element_type=jnp.float32
    )
    return (numerator, denominator + jnp.sum(weight, axis=-1))


def fold_keys(running, queries, key_rows, value_rows, usable):
    key_count = key_rows.shape[0]
    block_rows = max(
        (divisor for divisor in range(1, min(key_count, 2048) + 1) if key_count % divisor == 0)
    )
    step_count = key_count // block_rows
    if step_count == 1:
        return attend_block(running, queries, key_rows, value_rows, usable)

    def scan_step(state, members):
        return (attend_block(state, queries, members[0], members[1], members[2]), None)

    stacked = (
        key_rows.reshape(step_count, block_rows, key_rows.shape[1], key_rows.shape[2]),
        value_rows.reshape(step_count, block_rows, value_rows.shape[1], value_rows.shape[2]),
        usable.reshape(step_count, 1, block_rows),
    )
    running, _ = lax.scan(scan_step, running, stacked)
    return running


def compact_rows(mask_row):
    ranks = jnp.cumsum(mask_row) - 1
    target = jnp.where(mask_row == 1, ranks, MOST_KEEP)
    spots = (
        jnp.zeros((MOST_KEEP,), jnp.int32)
        .at[target]
        .set(jnp.arange(mask_row.shape[0], dtype=jnp.int32), mode="drop")
    )
    return (spots, jnp.sum(mask_row))


def head_totals(kept_part, cross_part):
    return lax.psum((kept_part, cross_part), "mp")


def body(
    patches,
    keep_mask,
    segment,
    w_query,
    w_key,
    w_value,
    w_out,
    w_cross_query,
    w_cross_out,
    w_up,
    w_down,
):
    rows_dev = patches.shape[0]
    devices_tm = lax.axis_size("tm")
    my_index = lax.axis_index("tm")
    head_width = w_query.shape[1]
    heads_local = head_width // HD
    kept_counts = jnp.sum(keep_mask.reshape(devices_tm, rows_dev), axis=1)
    padded_mask = jnp.concatenate(
        [jnp.zeros((rows_dev,), jnp.int32), keep_mask, jnp.zeros((rows_dev,), jnp.int32)]
    )
    padded_segment = jnp.concatenate(
        [jnp.full((rows_dev,), -1, jnp.int32), segment, jnp.full((rows_dev,), -1, jnp.int32)]
    )
    near_mask = lax.dynamic_slice_in_dim(padded_mask, my_index * rows_dev, 3 * rows_dev, 0).reshape(
        3, rows_dev
    )
    near_segment = lax.dynamic_slice_in_dim(
        padded_segment, my_index * rows_dev, 3 * rows_dev, 0
    ).reshape(3, rows_dev)
    positions, near_counts = jax.vmap(compact_rows)(near_mask)
    near_segments = jnp.take_along_axis(near_segment, positions, axis=1)
    near_usable = jnp.arange(MOST_KEEP, dtype=jnp.int32)[None, :] < near_counts[:, None]
    own_mask = near_mask[1]
    own_segment = near_segment[1]
    own_positions = positions[1]
    normed = norm_rows(patches).astype(jnp.bfloat16)
    key_all = jnp.dot(normed, w_key, preferred_element_type=jnp.float32).astype(jnp.bfloat16)
    value_all = jnp.dot(normed, w_value, preferred_element_type=jnp.float32).astype(jnp.bfloat16)
    cross_query = jnp.dot(normed, w_cross_query, preferred_element_type=jnp.float32).astype(
        jnp.bfloat16
    )
    kept_patches = patches[own_positions]
    kept_query = jnp.dot(normed[own_positions], w_query, preferred_element_type=jnp.float32).astype(
        jnp.bfloat16
    )
    kept_key = key_all[own_positions]
    kept_value = value_all[own_positions]
    span_pairs = jnp.concatenate([kept_key, kept_value], axis=1)
    window = with_halo(span_pairs, (("tm", 0),), MOST_KEEP)
    span_usable = near_usable.reshape(-1)[None, :] & (
        near_segments.reshape(-1)[None, :] == own_segment[:, None]
    )
    cross_heads = split_heads(cross_query)
    cross_start = (
        jnp.zeros((rows_dev, heads_local, HD), jnp.float32),
        jnp.zeros((rows_dev, heads_local), jnp.float32),
    )
    cross_num, cross_den = attend_block(
        cross_start,
        cross_heads,
        split_heads(window[:, :head_width]),
        split_heads(window[:, head_width:]),
        span_usable,
    )
    self_weight = jnp.exp(
        jnp.sum(cross_heads.astype(jnp.float32) * split_heads(key_all).astype(jnp.float32), axis=-1)
        * HD ** (-0.5)
    )
    self_rounded = lax.optimization_barrier(self_weight.astype(jnp.bfloat16)).astype(jnp.float32)
    cross_num = cross_num + self_rounded[:, :, None] * split_heads(value_all).astype(jnp.float32)
    cross_den = cross_den + self_weight
    cross_out = (
        (cross_num / cross_den[:, :, None]).astype(jnp.bfloat16).reshape(rows_dev, head_width)
    )
    cross_part = jnp.dot(cross_out, w_cross_out, preferred_element_type=jnp.float32)
    home_query = split_heads(kept_query)
    kept_start = (
        jnp.zeros((MOST_KEEP, heads_local, HD), jnp.float32),
        jnp.zeros((MOST_KEEP, heads_local), jnp.float32),
    )
    pieces = (
        lax.all_gather(kept_key, "tm", axis=0, tiled=True),
        lax.all_gather(kept_value, "tm", axis=0, tiled=True),
    )
    ranks = jnp.arange(pieces[0].shape[0], dtype=jnp.int32)
    usable = (ranks % MOST_KEEP < kept_counts[ranks // MOST_KEEP])[None, :]
    kept_num, kept_den = fold_keys(
        kept_start, home_query, split_heads(pieces[0]), split_heads(pieces[1]), usable
    )
    kept_rows = kept_num.shape[0]
    kept_out = (kept_num / kept_den[:, :, None]).astype(jnp.bfloat16).reshape(kept_rows, head_width)
    kept_part = jnp.dot(kept_out, w_out, preferred_element_type=jnp.float32)
    attn_total, cross_total = head_totals(kept_part, cross_part)
    hidden_rows = kept_patches.astype(jnp.float32) + attn_total
    normed_hidden = norm_rows(hidden_rows).astype(jnp.bfloat16)
    gated = jax.nn.gelu(
        jnp.dot(normed_hidden, w_up, preferred_element_type=jnp.float32), approximate=True
    ).astype(jnp.bfloat16)
    down_total = lax.psum(
        jnp.dot(gated, w_down, preferred_element_type=jnp.float32).astype(jnp.bfloat16), "mp"
    ).astype(jnp.float32)
    result_rows = (hidden_rows + down_total).astype(jnp.bfloat16)
    pruned_rows = (patches.astype(jnp.float32) + cross_total).astype(jnp.bfloat16)
    local_rank = jnp.clip(jnp.cumsum(own_mask) - 1, 0, MOST_KEEP - 1)
    return jnp.where(own_mask[:, None] == 1, result_rows[local_rank], pruned_rows)


def solution(mesh):
    placed = (
        P("tm", None),
        P(),
        P(),
        P(None, "mp"),
        P(None, "mp"),
        P(None, "mp"),
        P("mp", None),
        P(None, "mp"),
        P("mp", None),
        P(None, "mp"),
        P("mp", None),
    )
    return jax.shard_map(body, mesh=mesh, in_specs=placed, out_specs=P("tm", None), check_vma=False)
```

profile of v0, /device:TPU:1, one launch (start us, length us, event | category | flops | bytes accessed | tf_op | source)
XLA Modules:
  0.0 457.4 jit_solution(9372902527415595314)
XLA Ops:
  9.4 22.6 %scatter_fusion = s32[3,72]{1,0:T(4,128)S(1)} fusion(s32[3,72]{1,0:T(4,128)S(1)} %broadcast_in_dim.77, s32[480]{0:T(512)S(1)} %reshape.349, s32[480]{0:T(512)S(1)} %reshape.351), kind=kCustom, calls=%fused_computation.7 | custom fusion | bytes 9600 | tf_op jit(solution)/shard_map/vmap()/scatter | solution.py:72
  39.6 1.4 constant_dynamic-update-slice_fusion
  41.1 6.2 %collective-permute-start = (bf16[72,768]{1,0:T(8,128)(2,1)}, bf16[72,768]{1,0:T(8,128)(2,1)}, u32[]{:S(2)}, u32[]{:S(2)}) collective-permute-start(bf16[72,768]{1,0:T(8,128)(2,1)} %constant_dynamic-update-slice_fusion), channel_id=1, source_target_pairs={{0,2},{2,4},{4,6},{6,8},{8,10},{10,12},{12,14},{14,16},{16,18},{18... | collective-permute-start | bytes 331784 | tf_op jit(solution)/shard_map/ppermute | solution.py:15
  47.3 1.9 collective-permute-start.1
  50.8 1.6 concatenate.15
  58.1 3.5 gather_fusion.6
  64.0 54.9 %gather_fusion.2 = s32[9216]{0:T(1024)S(1)} fusion(s32[128]{0:T(128)S(1)} %reduce_sum.83, s32[9216]{0:T(1024)S(1)} %broadcast_clamp_fusion), kind=kCustom, calls=%fused_computation.2 | custom fusion | bytes 110592 | tf_op jit(solution)/shard_map/gather | solution.py:168
  121.2 2.1 fusion.69
  123.5 1.5 fusion.26
  126.1 39.9 %all-gather.7.cloned.1.call-done = bf16[9216,384]{1,0:T(8,128)(2,1)} async-done(((bf16[72,384]{1,0:T(8,128)(2,1)}), bf16[9216,384]{1,0:T(8,128)(2,1)}) %all-gather.7.cloned.1.call-update) | async-done | bytes 7077904 | tf_op jit(solution)/shard_map/all_gather | solution.py:164
  166.0 22.0 %reshape.364 = bf16[6,1536,6,64]{3,2,1,0:T(8,128)(2,1)} reshape(bf16[9216,384]{1,0:T(8,128)(2,1)} %all-gather.7.cloned.1.call-done) | data formatting | bytes 14155776 | tf_op jit(solution)/shard_map/reshape;reshape | solution.py:58
  188.0 19.1 %copy.27 = bf16[6,1536,6,64]{1,3,2,0:T(8,128)(2,1)} copy(bf16[6,1536,6,64]{3,2,1,0:T(8,128)(2,1)} %reshape.364) | data formatting | bytes 14155776
  207.1 85.2 %all-gather.5.cloned.1.call-done = bf16[9216,384]{1,0:T(8,128)(2,1)} async-done(((bf16[72,384]{1,0:T(8,128)(2,1)}), bf16[9216,384]{1,0:T(8,128)(2,1)}) %all-gather.5.cloned.1.call-update) | async-done | bytes 7077904 | tf_op jit(solution)/shard_map/all_gather | solution.py:165
  292.3 22.0 %reshape.363 = bf16[6,1536,6,64]{3,2,1,0:T(8,128)(2,1)} reshape(bf16[9216,384]{1,0:T(8,128)(2,1)} %all-gather.5.cloned.1.call-done) | data formatting | bytes 14155776 | tf_op jit(solution)/shard_map/reshape;reshape | solution.py:59
  314.3 19.1 %copy.26 = bf16[6,1536,6,64]{1,3,2,0:T(8,128)(2,1)} copy(bf16[6,1536,6,64]{3,2,1,0:T(8,128)(2,1)} %reshape.363) | data formatting | bytes 14155776
  333.4 32.0 %while.13 = (s32[]{:T(128)}, f32[72,6,64]{0,2,1:T(8,128)S(1)}, f32[72,6]{0,1:T(8,128)S(1)}, bf16[6,1536,6,64]{1,3,2,0:T(8,128)(2,1)}, pred[6,1,1536]{2,1,0:T(4,1...) while((s32[]{:T(128)}, f32[72,6,64]{0,2,1:T(8,128)S(1)}, ...), condition=%wide.region_8.9_spmd.clone, body=%wide.region_6.8_spmd.clone.sunk | while | flops 172579248 | bytes 5302636 | solution.py:62
  333.4 3.1 fusion.100
  336.5 2.2 fusion.101
  338.8 3.1 fusion.100
  341.9 2.2 fusion.101
  344.1 3.1 fusion.100
  347.2 2.2 fusion.101
  349.4 3.1 fusion.100
  352.5 2.2 fusion.101
  354.8 3.1 fusion.100
  357.9 2.2 fusion.101
  360.1 3.1 fusion.100
  363.2 2.2 fusion.101
  365.5 2.0 fusion.70
  368.7 40.0 %all-reduce.8.cloned.1.call-done = (f32[72,768]{1,0:T(8,128)}, f32[160,768]{1,0:T(8,128)}) async-done(((f32[72,768]{1,0:T(8,128)}, f32[160,768]{1,0:T(8,128)}), (f32[72,768]{1,0:T(8,128)}, f32[160,768]{1,0:T(8,128)})) %all-reduce.8.cloned.1.call-update) | async-done | bytes 712720 | tf_op jit(solution)/shard_map/psum | solution.py:78
  410.9 3.5 convolution_convert_fusion.3
  414.5 33.7 %all-reduce.6.cloned.1.call-done = bf16[72,768]{1,0:T(8,128)(2,1)} async-done(((bf16[72,768]{1,0:T(8,128)(2,1)}), bf16[72,768]{1,0:T(8,128)(2,1)}) %all-reduce.6.cloned.1.call-update) | async-done | bytes 110608 | tf_op jit(solution)/shard_map/psum | solution.py:181
  (127 shorter events, 29.8 us)
Async XLA Ops:
  6.5 404.4 %copy-start = (bf16[1536,768]{1,0:T(8,128)(2,1)S(1)}, bf16[1536,768]{1,0:T(8,128)(2,1)}, u32[]{:S(2)}) copy-start(bf16[1536,768]{1,0:T(8,128)(2,1)} %param.23) | copy-start | bytes 7077892
  6.5 159.5 %all-gather.7.cloned.1.call-start = ((), (), s32[]{:S(2)}) async-start(), calls=%async_computation.2 | async-start | bytes 7133184 | tf_op jit(solution)/shard_map/all_gather | solution.py:164
  9.4 22.7 %copy-start.1 = (bf16[160,768]{1,0:T(8,128)(2,1)S(1)}, bf16[160,768]{1,0:T(8,128)(2,1)}, u32[]{:S(2)}) copy-start(bf16[160,768]{1,0:T(8,128)(2,1)} %param.13) | copy-start | bytes 737284
  32.1 18.5 %copy-start.8 = (s32[1024]{0:T(1024)}, s32[1024]{0:T(1024)S(1)}, u32[]{:S(2)}) copy-start(s32[1024]{0:T(1024)S(1)} %pad_clamp_fusion.1) | copy-start | bytes 12292
  32.5 18.1 %copy-start.6 = (s32[20480]{0:T(1024)S(1)}, s32[20480]{0:T(1024)}, u32[]{:S(2)}) copy-start(s32[20480]{0:T(1024)} %param.14) | copy-start | bytes 245764
  35.4 256.9 %all-gather.5.cloned.1.call-start = ((), (), s32[]{:S(2)}) async-start(), calls=%async_computation.1 | async-start | bytes 7133184 | tf_op jit(solution)/shard_map/all_gather | solution.py:165
  38.1 370.6 %all-reduce.8.cloned.1.call-start = ((), (), s32[]{:S(2)}) async-start(), calls=%async_computation.3 | async-start | bytes 1425408 | tf_op jit(solution)/shard_map/psum | solution.py:78
  41.1 78.2 %collective-permute-start = (bf16[72,768]{1,0:T(8,128)(2,1)}, bf16[72,768]{1,0:T(8,128)(2,1)}, u32[]{:S(2)}, u32[]{:S(2)}) collective-permute-start(bf16[72,768]{1,0:T(8,128)(2,1)} %constant_dynamic-update-slice_fusion), channel_id=1, source_target_pairs={{0,2},{2,4},{4,6},{6,8},{8,10},{10,12},{12,14},{14,16},{16,18},{18... | collective-permute-start | bytes 331784 | tf_op jit(solution)/shard_map/ppermute | solution.py:15
  47.3 72.0 %collective-permute-start.1 = (bf16[72,768]{1,0:T(8,128)(2,1)}, bf16[72,768]{1,0:T(8,128)(2,1)}, u32[]{:S(2)}, u32[]{:S(2)}) collective-permute-start(bf16[72,768]{1,0:T(8,128)(2,1)} %constant_dynamic-update-slice_fusion), channel_id=1, source_target_pairs={{2,0},{4,2},{6,4},{8,6},{10,8},{12,10},{14,12},{16,14},{18,16},{20... | collective-permute-start | bytes 331784 | tf_op jit(solution)/shard_map/ppermute | solution.py:18
  64.0 54.9 %copy-start.9 = (s32[160]{0:T(256)S(1)}, s32[160]{0:T(256)}, u32[]{:S(2)}) copy-start(s32[160]{0:T(256)} %slice.45) | copy-start | bytes 1924
  64.0 55.2 %copy-start.3 = (f32[160,384]{0,1:T(8,128)S(1)}, f32[160,384]{0,1:T(8,128)}, u32[]{:S(2)}) copy-start(f32[160,384]{0,1:T(8,128)} %copy.31) | copy-start | bytes 737284
  123.5 1.5 copy-start.4
  314.3 19.1 %copy-start.7 = (bf16[72,384]{0,1:T(8,128)(2,1)S(1)}, bf16[72,384]{0,1:T(8,128)(2,1)}, u32[]{:S(2)}) copy-start(bf16[72,384]{0,1:T(8,128)(2,1)} %copy.25) | copy-start | bytes 165892
  367.5 80.7 %all-reduce.6.cloned.1.call-start = ((), (), s32[]{:S(2)}) async-start(), calls=%async_computation | async-start | bytes 221184 | tf_op jit(solution)/shard_map/psum | solution.py:181
  410.9 37.3 %copy-start.2 = (f32[72,768]{1,0:T(8,128)S(1)}, f32[72,768]{1,0:T(8,128)}, u32[]{:S(2)}) copy-start(f32[72,768]{1,0:T(8,128)} %get-tuple-element.97) | copy-start | bytes 663556
  414.5 35.6 %copy-start.5 = (f32[160,768]{1,0:T(8,128)S(1)}, f32[160,768]{1,0:T(8,128)}, u32[]{:S(2)}) copy-start(f32[160,768]{1,0:T(8,128)} %get-tuple-element.98) | copy-start | bytes 1474564
Sparse Core Ops, SparseCore 0:
  35.5 130.4 all-gather.6
  169.7 122.5 all-gather.4
  367.6 41.0 all-reduce.7
  414.6 33.5 all-reduce.5
where the time goes:
time: 461 us; the launch traced here: 457 us
  waiting for transfers between devices  199 us (43%)
  local copies, waits for them, and re-layouts  181 us (39%)
  matrix products  47.3 us (10%)
  between operations  13.5 us (3%)
  starting transfers between devices  8.25 us (2%)
  other arithmetic  7.84 us (2%)
    all_gather x1, waiting for transfers between devices, body(): lax.all_gather(kept_value, 'tm', axis=0, tiled=True)  85.2 us
    gather x1, local copies, waits for them, and re-layouts, body(): usable = (ranks % MOST_KEEP < kept_counts[ranks // MOST_KEEP])[None, :]  54.9 us
    psum x1, waiting for transfers between devices, head_totals(): return lax.psum((kept_part, cross_part), 'mp')  40 us
    all_gather x1, waiting for transfers between devices, body(): lax.all_gather(kept_key, 'tm', axis=0, tiled=True)  39.9 us
    unnamed x24, local copies, waits for them, and re-layouts  39.7 us
    psum x1, waiting for transfers between devices, body(): lax.psum(jnp.dot(gated, w_down, preferred_element_type=jnp.float32).astyp...  33.7 us
    scatter x2, local copies, waits for them, and re-layouts, compact_rows(): spots = jnp.zeros((MOST_KEEP,), jnp.int32).at[target].set(jnp.arange(mask...  22.7 us
    another operation x1, local copies, waits for them, and re-layouts, fold_keys(): key_rows.reshape(step_count, block_rows, key_rows.shape[1], key_rows.shap...  22 us
  transfers between devices with their start and end apart: 6, of which 4 were waited for; matrix products, arithmetic and copies ran while one was open for 27% of the time, Pallas kernels for 0%

commit v1 on v0

v1 whole, which is shorter than its diff:
```python
import functools

import jax
import jax.numpy as jnp
from jax import lax
from jax.experimental import pallas as pl
from jax.experimental.pallas import tpu as pltpu
from jax.sharding import PartitionSpec as P

KEPT = 48
EDGE = 16
WINDOW = KEPT + 2 * EDGE
F32 = jnp.float32
BF16 = jnp.bfloat16


def norm_rows(values):
    values = values.astype(F32)
    center = values - jnp.mean(values, axis=-1, keepdims=True)
    return center * lax.rsqrt(jnp.mean(center * center, axis=-1, keepdims=True) + 1e-05)


def dot(a, b):
    return jnp.dot(a, b, preferred_element_type=F32)


def dot_t(a, b):
    return lax.dot_general(a, b, (((1,), (1,)), ((), ())), preferred_element_type=F32)


def dot_0(a, b):
    return lax.dot_general(a, b, (((0,), (0,)), ((), ())), preferred_element_type=F32)


def iota(shape, dim):
    return lax.broadcasted_iota(jnp.int32, shape, dim)


def attend_pair(queries, keys, values, usable):
    rows = queries.shape[0]
    low = iota((rows, 128), 1) < 64
    zero = jnp.zeros_like(queries)
    both = jnp.concatenate([jnp.where(low, queries, zero), jnp.where(low, zero, queries)], axis=0)
    weight = jnp.exp(dot_t(both, keys))
    if usable is not None:
        weight = jnp.where(usable, weight, 0.0)
    ones = jnp.ones((keys.shape[0], 128), BF16)
    total = dot(weight.astype(BF16), jnp.concatenate([values, ones], axis=1))
    numerator = jnp.where(low, total[:rows, :128], total[rows:, :128])
    denominator = jnp.where(low, total[:rows, 128:], total[rows:, 128:])
    return numerator, denominator


def kernel(
    nx,
    nz,
    patches_ref,
    mask_ref,
    seg_ref,
    wq_hbm,
    wk_hbm,
    wv_hbm,
    wo_hbm,
    wcq_hbm,
    wco_hbm,
    wu_hbm,
    wd_hbm,
    out_ref,
    wproj,
    wo,
    wco,
    wu,
    wd,
    xwin,
    lwin,
    rwin,
    kvbuf,
    qbuf,
    rsout,
    rsin,
    keys,
    attn_out,
    attn_in,
    cross_out,
    cross_in,
    down_out,
    down_in,
    result,
    left_result,
    right_result,
    wsem,
    ssem,
    rsem,
):
    ntm = nx * nz * 4
    rows_dev, width = patches_ref.shape
    half = wq_hbm.shape[1]
    me = lax.axis_index("tm")
    mp = lax.axis_index("mp")
    core = lax.rem(me, 2)
    yh = lax.rem(me // 2, 2)
    z = lax.rem(me // 4, nz)
    x = me // (4 * nz)
    sibling = me + 1 - 2 * core
    ypart = me + 2 - 4 * yh
    right = lax.rem(me + 1, ntm)
    left = lax.rem(me + ntm - 1, ntm)
    zpeer = [me + 4 * (lax.rem(z + k, nz) - z) for k in range(nz)]
    xpeer = [me + 4 * nz * (lax.rem(x + k, nx) - x) for k in range(nx)]

    weights = [
        (wq_hbm, wproj.at[:, 0:half]),
        (wk_hbm, wproj.at[:, half : 2 * half]),
        (wv_hbm, wproj.at[:, 2 * half : 3 * half]),
        (wcq_hbm, wproj.at[:, 3 * half : 4 * half]),
        (wco_hbm, wco),
        (wo_hbm, wo),
        (wu_hbm, wu),
        (wd_hbm, wd),
    ]
    loads = []
    for i, (source, target) in enumerate(weights):
        load = pltpu.make_async_copy(source, target, wsem.at[i])
        load.start()
        loads.append(load)

    barrier = pltpu.get_barrier_semaphore()
    greeted = [(sibling, mp), (ypart, mp), (right, mp), (left, mp), (me, 1 - mp)]
    greeted += [(peer, mp) for peer in zpeer[1:]] + [(peer, mp) for peer in xpeer[1:]]
    for target in greeted:
        pl.semaphore_signal(
            barrier, inc=1, device_id=target, device_id_type=pl.DeviceIdType.MESH
        )

    counter = [0]
    started = []

    def send(source, target, where):
        i = counter[0]
        counter[0] += 1
        copy = pltpu.make_async_remote_copy(
            src_ref=source,
            dst_ref=target,
            send_sem=ssem.at[i],
            recv_sem=rsem.at[i],
            device_id=where,
            device_id_type=pl.DeviceIdType.MESH,
        )
        copy.start()
        started.append(copy)
        return copy

    mask = mask_ref[...].astype(F32)
    before = jnp.where(iota(mask.shape, 0) < me, mask, 0.0)
    base = jnp.sum(jnp.sum(before, axis=1, keepdims=True), axis=0, keepdims=True)
    base = base - (KEPT * me).astype(F32)
    own_mask = mask_ref[pl.ds(me, 1), :].astype(F32)
    left_mask = jnp.where(me > 0, mask_ref[pl.ds(left, 1), :].astype(F32), 0.0)
    right_mask = jnp.where(me < ntm - 1, mask_ref[pl.ds(right, 1), :].astype(F32), 0.0)
    own_seg = seg_ref[pl.ds(me, 1), :].astype(F32) + 1.0
    left_seg = seg_ref[pl.ds(left, 1), :].astype(F32) + 1.0
    right_seg = seg_ref[pl.ds(right, 1), :].astype(F32) + 1.0
    earlier = (iota((rows_dev, rows_dev), 0) < iota((rows_dev, rows_dev), 1)).astype(F32)
    earlier = earlier.astype(BF16)

    def window(mask_row, base_row):
        rank = dot(jnp.broadcast_to(mask_row, (16, rows_dev)).astype(BF16), earlier)[0:1]
        slot = jnp.where(mask_row > 0.5, rank + base_row + float(EDGE), -1.0)
        grid = iota((WINDOW, rows_dev), 0).astype(F32)
        return jnp.where(grid == slot, 1.0, 0.0).astype(BF16)

    own_place = window(own_mask, base)
    patches = patches_ref[...]
    xwin[...] = dot(own_place, patches).astype(BF16)

    pl.semaphore_wait(barrier, len(greeted))

    edge_right = send(
        xwin.at[WINDOW - EDGE : WINDOW], lwin.at[WINDOW - EDGE : WINDOW], (right, mp)
    )
    edge_left = send(xwin.at[0:EDGE], rwin.at[0:EDGE], (left, mp))

    own_count = jnp.sum(own_mask, axis=1, keepdims=True)
    left_count = jnp.sum(left_mask, axis=1, keepdims=True)
    left_place = window(left_mask, base - left_count + float(KEPT))
    right_place = window(right_mask, base + own_count - float(KEPT))

    def key_segments(mask_place, seg_row):
        return dot_t(jnp.broadcast_to(seg_row, (16, rows_dev)).astype(BF16), mask_place)[0:1]

    key_seg = jnp.concatenate(
        [
            jnp.where(own_mask > 0.5, own_seg, 0.0),
            key_segments(left_place, left_seg),
            key_segments(right_place, right_seg),
        ],
        axis=1,
    )
    nkeys = rows_dev + 2 * WINDOW
    same = iota((rows_dev, rows_dev), 0) == iota((rows_dev, rows_dev), 1)
    seg_diag = jnp.where(same, own_seg, 0.0).astype(BF16)
    mask_diag = jnp.where(same, own_mask, 0.0).astype(BF16)
    query_seg = dot(seg_diag, jnp.ones((rows_dev, nkeys), BF16))
    usable = (query_seg == key_seg) | (
        iota((rows_dev, nkeys), 0) == iota((rows_dev, nkeys), 1)
    )
    usable = jnp.where(usable, 1.0, 0.0)
    usable = jnp.concatenate([usable, usable], axis=0) > 0.5
    kept_column = dot(mask_diag, jnp.ones((rows_dev, width), BF16)) > 0.5
    normed = norm_rows(patches).astype(BF16)

    edge_right.wait_recv()
    edge_left.wait_recv()
    own_rows = xwin[EDGE : EDGE + KEPT].astype(F32)
    kept = jnp.concatenate(
        [
            own_rows[:EDGE]
            + jnp.where(me > 0, lwin[WINDOW - EDGE : WINDOW].astype(F32), 0.0),
            own_rows[EDGE : KEPT - EDGE],
            own_rows[KEPT - EDGE :] + jnp.where(me < ntm - 1, rwin[0:EDGE].astype(F32), 0.0),
        ],
        axis=0,
    )
    for load in loads[:3]:
        load.wait()
    qkv = dot(norm_rows(kept).astype(BF16), wproj[:, : 3 * half])
    qbuf[0:KEPT] = (qkv[:, :half].astype(BF16).astype(F32) * 0.125).astype(BF16)
    kvbuf[0:KEPT] = qkv[:, half:].astype(BF16)

    def slots(ref, first, count):
        return ref.at[first * KEPT : (first + count) * KEPT]

    kv_y = send(slots(kvbuf, 0, 1), slots(kvbuf, nx, 1), (ypart, mp))
    kv_x = [
        send(slots(kvbuf, 0, 1), slots(kvbuf, nx - k, 1), (xpeer[k], mp)) for k in range(1, nx)
    ]
    far_first = sorted(range(1, nz), key=lambda k: -min(k, nz - k))
    q_z = [send(slots(qbuf, 0, 1), slots(qbuf, nz - k, 1), (zpeer[k], mp)) for k in far_first]
    kv_s = [send(slots(kvbuf, 0, 1), slots(kvbuf, 2 * nx, 1), (sibling, mp))]
    halo_right = send(xwin.at[0 : WINDOW - EDGE], lwin.at[0 : WINDOW - EDGE], (right, mp))
    halo_left = send(xwin.at[EDGE:WINDOW], rwin.at[EDGE:WINDOW], (left, mp))

    loads[3].wait()
    own_proj = dot(normed, wproj[:, half:])
    keys[0:rows_dev] = own_proj[:, : 2 * half].astype(BF16)
    cross_query = (own_proj[:, 2 * half :].astype(BF16).astype(F32) * 0.125).astype(BF16)

    kv_y.wait_recv()
    kv_x2 = [
        send(slots(kvbuf, nx, 1), slots(kvbuf, 2 * nx - k, 1), (xpeer[k], mp))
        for k in range(1, nx)
    ]

    halo_right.wait_recv()
    halo_left.wait_recv()
    near = jnp.concatenate([lwin[...], rwin[...]], axis=0)
    keys[rows_dev:nkeys] = dot(
        norm_rows(near).astype(BF16), wproj[:, half : 3 * half]
    ).astype(BF16)

    pairs = []

    def cross_pair(i):
        numerator, denominator = attend_pair(
            cross_query[:, 128 * i : 128 * (i + 1)],
            keys[:, 128 * i : 128 * (i + 1)],
            keys[:, half + 128 * i : half + 128 * (i + 1)],
            usable,
        )
        pairs.append((numerator / denominator).astype(BF16))

    npairs = half // 128
    for i in range(npairs):
        cross_pair(i)
        if i == 0:
            for copy in kv_x:
                copy.wait_recv()
            kv_s.append(send(slots(kvbuf, 1, nx - 1), slots(kvbuf, 2 * nx + 1, nx - 1), (sibling, mp)))
        if i == 1:
            for copy in kv_x2:
                copy.wait_recv()
            kv_s.append(send(slots(kvbuf, nx, nx), slots(kvbuf, 3 * nx, nx), (sibling, mp)))
    loads[4].wait()
    cross_out[...] = dot(jnp.concatenate(pairs, axis=1), wco[...]).astype(BF16)
    cross_move = send(cross_out, cross_in, (me, 1 - mp))

    for copy in q_z:
        copy.wait_recv()
    for copy in kv_s:
        copy.wait_recv()

    half_mod = lax.rem(iota((1, 128), 1), 64)

    def partials(queries):
        parts, dens = [], []
        for i in range(npairs):
            numerator, denominator = attend_pair(
                queries[:, 128 * i : 128 * (i + 1)],
                kvbuf[:, 128 * i : 128 * (i + 1)],
                kvbuf[:, half + 128 * i : half + 128 * (i + 1)],
                None,
            )
            parts.append(numerator)
            dens.append(denominator)
        packed = dens[0]
        for i in range(1, npairs):
            packed = jnp.where(half_mod >= 16 * i, dens[i], packed)
        return jnp.concatenate(parts + [packed], axis=1)

    rs_move = []
    quarter = nz // 4
    far = partials(qbuf[quarter * KEPT : (nz - quarter) * KEPT])
    rsout[quarter * KEPT : (nz - quarter) * KEPT] = far.astype(BF16)
    for k in far_first:
        if quarter <= k < nz - quarter:
            rs_move.append(send(slots(rsout, k, 1), slots(rsin, nz - k, 1), (zpeer[k], mp)))
    close = partials(
        jnp.concatenate([qbuf[(nz - quarter) * KEPT : nz * KEPT], qbuf[0 : quarter * KEPT]], axis=0)
    )
    rsout[(nz - quarter) * KEPT : nz * KEPT] = close[: quarter * KEPT].astype(BF16)
    rsout[0 : quarter * KEPT] = close[quarter * KEPT :].astype(BF16)
    for k in far_first:
        if not quarter <= k < nz - quarter:
            rs_move.append(send(slots(rsout, k, 1), slots(rsin, nz - k, 1), (zpeer[k], mp)))
    total = close[quarter * KEPT : (quarter + 1) * KEPT]

    cross_move.wait_recv()
    pruned = patches.astype(F32) + (cross_out[...].astype(F32) + cross_in[...].astype(F32))

    for copy in rs_move:
        copy.wait_recv()
    for k in range(1, nz):
        total = total + rsin[k * KEPT : (k + 1) * KEPT].astype(F32)
    low = iota((KEPT, 128), 1) < 64
    attention = []
    for i in range(npairs):
        first = total[:, half + 16 * i : half + 16 * i + 1]
        second = total[:, half + 64 + 16 * i : half + 64 + 16 * i + 1]
        attention.append(
            (total[:, 128 * i : 128 * (i + 1)] / jnp.where(low, first, second)).astype(BF16)
        )
    loads[5].wait()
    attn_out[...] = dot(jnp.concatenate(attention, axis=1), wo[...]).astype(BF16)
    attn_move = send(attn_out, attn_in, (me, 1 - mp))
    loads[6].wait()
    loads[7].wait()
    attn_move.wait_recv()
    hidden = kept + (attn_out[...].astype(F32) + attn_in[...].astype(F32))
    gated = jax.nn.gelu(dot(norm_rows(hidden).astype(BF16), wu[...]), approximate=True)
    down_out[...] = dot(gated.astype(BF16), wd[...]).astype(BF16)
    down_move = send(down_out, down_in, (me, 1 - mp))
    down_move.wait_recv()
    result[...] = (hidden + (down_out[...].astype(F32) + down_in[...].astype(F32))).astype(BF16)
    result_right = send(result.at[KEPT - EDGE : KEPT], left_result, (right, mp))
    result_left = send(result.at[0:EDGE], right_result, (left, mp))
    result_right.wait_recv()
    result_left.wait_recv()
    finished = jnp.concatenate([left_result[...], result[...], right_result[...]], axis=0)
    spread = dot_0(own_place, finished)
    out_ref[...] = jnp.where(kept_column, spread, pruned).astype(BF16)

    for copy in started:
        copy.wait_send()


def body(nx, nz, patches, keep_mask, segment, *weights):
    rows, width = patches.shape
    half = weights[0].shape[1]
    hidden = weights[6].shape[1]
    ntm = nx * nz * 4
    copies = 24 + 3 * (nx - 1) + 2 * (nz - 1)
    vmem = lambda *shape: pltpu.VMEM(shape, BF16)
    return pl.pallas_call(
        functools.partial(kernel, nx, nz),
        out_shape=jax.ShapeDtypeStruct((rows, width), BF16),
        in_specs=[pl.BlockSpec(memory_space=pltpu.VMEM)] * 3
        + [pl.BlockSpec(memory_space=pl.ANY)] * 8,
        out_specs=pl.BlockSpec(memory_space=pltpu.VMEM),
        scratch_shapes=[
            vmem(width, 4 * half),
            vmem(half, width),
            vmem(half, width),
            vmem(width, hidden),
            vmem(hidden, width),
            vmem(WINDOW, width),
            vmem(WINDOW, width),
            vmem(WINDOW, width),
            vmem(4 * nx * KEPT, 2 * half),
            vmem(nz * KEPT, half),
            vmem(nz * KEPT, half + 128),
            vmem(nz * KEPT, half + 128),
            vmem(rows + 2 * WINDOW, 2 * half),
            vmem(KEPT, width),
            vmem(KEPT, width),
            vmem(rows, width),
            vmem(rows, width),
            vmem(KEPT, width),
            vmem(KEPT, width),
            vmem(KEPT, width),
            vmem(EDGE, width),
            vmem(EDGE, width),
            pltpu.SemaphoreType.DMA((8,)),
            pltpu.SemaphoreType.DMA((copies,)),
            pltpu.SemaphoreType.DMA((copies,)),
        ],
        compiler_params=pltpu.CompilerParams(
            collective_id=0, has_side_effects=True, vmem_limit_bytes=48 * 1024 * 1024
        ),
    )(patches, keep_mask.reshape(ntm, rows), segment.reshape(ntm, rows), *weights)


def solution(mesh):
    placed = (
        P("tm", None),
        P(),
        P(),
        P(None, "mp"),
        P(None, "mp"),
        P(None, "mp"),
        P("mp", None),
        P(None, "mp"),
        P("mp", None),
        P(None, "mp"),
        P("mp", None),
    )
    ntm = mesh.shape["tm"]
    nx = 4 if ntm == 128 else 2
    return jax.shard_map(
        functools.partial(body, nx, ntm // (4 * nx)),
        mesh=mesh,
        in_specs=placed,
        out_specs=P("tm", None),
        check_vma=False,
    )
```

time: 461 us -> 63.3 us (0.14)
  waiting for transfers between devices: 199 us -> 0 us
  local copies, waits for them, and re-layouts: 181 us -> 9.98 us
  Pallas kernels: 0 us -> 52.8 us
  matrix products: 47.3 us -> 0 us
  between operations: 13.5 us -> 0.04 us
  starting transfers between devices: 8.25 us -> 0 us
  other arithmetic: 7.84 us -> 0 us
    all_gather x2 -> x0, waiting for transfers between devices: 125 us -> none  [the longest x1 85.2 us: body(): lax.all_gather(kept_value, 'tm', axis=0, tiled=True)]
    psum x2 -> x0, waiting for transfers between devices: 73.7 us -> none  [the longest x1 40 us: head_totals(): return lax.psum((kept_part, cross_part), 'mp')]
    gather x9 -> x0, local copies, waits for them, and re-layouts: 64.4 us -> none  [the longest x1 54.9 us: body(): usable = (ranks % MOST_KEEP < kept_counts[ranks // MOST_KEEP])[None, :]]
    pallas_call x0 -> x1, Pallas kernels: none -> 52.8 us  [body(): pl.pallas_call(functools.partial(kernel, nx, nz), out_shape=jax.ShapeDtyp...]
    dot_general x21 -> x0, matrix products: 47.3 us -> none  [the longest x7 20.7 us: attend_block(): jnp.einsum('rhe,mhe->rhm', queries, key_rows, preferred_element_type=jnp....]
    another operation x10 -> x0, local copies, waits for them, and re-layouts: 44.3 us -> none  [the longest x1 22 us: fold_keys(): key_rows.reshape(step_count, block_rows, key_rows.shape[1], key_rows.shap...]
    unnamed x24 -> x15, local copies, waits for them, and re-layouts: 39.7 us -> 8.02 us
    scatter x2 -> x0, local copies, waits for them, and re-layouts: 22.7 us -> none  [compact_rows(): spots = jnp.zeros((MOST_KEEP,), jnp.int32).at[target].set(jnp.arange(mask...]
  transfers between devices with their start and end apart: 6 -> 0, of which waited for: 4 -> 0; matrix products, arithmetic and copies ran while one was open for 27% -> 0% of each run, Pallas kernels for 0% -> 0%
where the time goes in v1:
time: 63.3 us; the launch traced here: 62.8 us
  Pallas kernels  52.8 us (83%)
  local copies, waits for them, and re-layouts  9.98 us (16%)
    pallas_call x1, Pallas kernels, body(): pl.pallas_call(functools.partial(kernel, nx, nz), out_shape=jax.ShapeDtyp...  52.8 us
    unnamed x15, local copies, waits for them, and re-layouts  8.02 us

profile of v1, /device:TPU:1, one launch (start us, length us, event | category | flops | bytes accessed | tf_op | source)
XLA Modules:
  0.0 62.8 jit_solution(1293846362184303834)
XLA Ops:
  0.0 1.0 %reshape.6.mask_ref = s32[128,160]{1,0:T(8,128)S(1)} reshape(s32[20480]{0:T(1024)} %param.12) | data formatting | bytes 163840 | tf_op jit(solution)/shard_map/reshape | solution.py:409
  1.0 1.0 %reshape.7.seg_ref = s32[128,160]{1,0:T(8,128)S(1)} reshape(s32[20480]{0:T(1024)} %param.13) | data formatting | bytes 163840 | tf_op jit(solution)/shard_map/reshape | solution.py:409
  2.0 0.0 copy-start
  2.0 1.1 %copy-done = bf16[768,384]{1,0:T(8,128)(2,1)S(1)} copy-done((bf16[768,384]{1,0:T(8,128)(2,1)S(1)}, bf16[768,384]{1,0:T(8,128)(2,1)}, u32[]{:S(2)}) %copy-start) | copy-done | bytes 589848
  3.1 0.0 copy-start.1
  3.1 1.1 %copy-done.1 = bf16[768,384]{1,0:T(8,128)(2,1)S(1)} copy-done((bf16[768,384]{1,0:T(8,128)(2,1)S(1)}, bf16[768,384]{1,0:T(8,128)(2,1)}, u32[]{:S(2)}) %copy-start.1) | copy-done | bytes 589848
  4.1 0.0 copy-start.2
  4.1 1.1 %copy-done.2 = bf16[768,384]{1,0:T(8,128)(2,1)S(1)} copy-done((bf16[768,384]{1,0:T(8,128)(2,1)S(1)}, bf16[768,384]{1,0:T(8,128)(2,1)}, u32[]{:S(2)}) %copy-start.2) | copy-done | bytes 589848
  5.2 0.0 copy-start.3
  5.2 1.1 %copy-done.3 = bf16[384,768]{1,0:T(8,128)(2,1)S(1)} copy-done((bf16[384,768]{1,0:T(8,128)(2,1)S(1)}, bf16[384,768]{1,0:T(8,128)(2,1)}, u32[]{:S(2)}) %copy-start.3) | copy-done | bytes 589848
  6.2 0.0 copy-start.4
  6.2 1.1 %copy-done.4 = bf16[768,384]{1,0:T(8,128)(2,1)S(1)} copy-done((bf16[768,384]{1,0:T(8,128)(2,1)S(1)}, bf16[768,384]{1,0:T(8,128)(2,1)}, u32[]{:S(2)}) %copy-start.4) | copy-done | bytes 589848
  7.3 0.0 copy-start.5
  7.3 1.1 %copy-done.5 = bf16[384,768]{1,0:T(8,128)(2,1)S(1)} copy-done((bf16[384,768]{1,0:T(8,128)(2,1)S(1)}, bf16[384,768]{1,0:T(8,128)(2,1)}, u32[]{:S(2)}) %copy-start.5) | copy-done | bytes 589848
  8.4 0.0 copy-start.6
  8.4 0.9 %copy-done.6 = bf16[160,768]{1,0:T(8,128)(2,1)S(1)} copy-done((bf16[160,768]{1,0:T(8,128)(2,1)S(1)}, bf16[160,768]{1,0:T(8,128)(2,1)}, u32[]{:S(2)}) %copy-start.6) | copy-done | bytes 245784
  9.3 52.8 %shard_map.109 = bf16[160,768]{1,0:T(8,128)(2,1)S(1)} custom-call(bf16[160,768]{1,0:T(8,128)(2,1)S(1)} %copy-done.6, s32[128,160]{1,0:T(8,128)S(1)} %reshape.6.mask_ref, s32[128,160]{1,0:T(8,128)S(1)} %reshape.7.seg_ref, bf16[768,384]{1,0:T(8,128)(2,1)S(1)} %copy-done, bf16[768,384]{1,0:T(8,128)(2,1)S(1)} %copy-done.1, bf16[768,384]{1,0:T(8,128)(2,1)S(1)} %copy-done.2, ...), custom_call_target="tpu_custom_call" | custom-call | tf_op jit(solution)/shard_map/pallas_call | solution.py:373
  62.1 0.7 %copy.13 = bf16[160,768]{1,0:T(8,128)(2,1)} copy(bf16[160,768]{1,0:T(8,128)(2,1)S(1)} %shard_map.109) | data formatting | bytes 491520
Async XLA Ops:
  2.0 1.1 %copy-start = (bf16[768,384]{1,0:T(8,128)(2,1)S(1)}, bf16[768,384]{1,0:T(8,128)(2,1)}, u32[]{:S(2)}) copy-start(bf16[768,384]{1,0:T(8,128)(2,1)} %wq_hbm.1) | copy-start | bytes 1769476
  3.1 1.1 %copy-start.1 = (bf16[768,384]{1,0:T(8,128)(2,1)S(1)}, bf16[768,384]{1,0:T(8,128)(2,1)}, u32[]{:S(2)}) copy-start(bf16[768,384]{1,0:T(8,128)(2,1)} %wk_hbm.1) | copy-start | bytes 1769476
  4.1 1.1 %copy-start.2 = (bf16[768,384]{1,0:T(8,128)(2,1)S(1)}, bf16[768,384]{1,0:T(8,128)(2,1)}, u32[]{:S(2)}) copy-start(bf16[768,384]{1,0:T(8,128)(2,1)} %wv_hbm.1) | copy-start | bytes 1769476
  5.2 1.1 %copy-start.3 = (bf16[384,768]{1,0:T(8,128)(2,1)S(1)}, bf16[384,768]{1,0:T(8,128)(2,1)}, u32[]{:S(2)}) copy-start(bf16[384,768]{1,0:T(8,128)(2,1)} %wo_hbm.1) | copy-start | bytes 1769476
  6.2 1.1 %copy-start.4 = (bf16[768,384]{1,0:T(8,128)(2,1)S(1)}, bf16[768,384]{1,0:T(8,128)(2,1)}, u32[]{:S(2)}) copy-start(bf16[768,384]{1,0:T(8,128)(2,1)} %wcq_hbm.1) | copy-start | bytes 1769476
  7.3 1.1 %copy-start.5 = (bf16[384,768]{1,0:T(8,128)(2,1)S(1)}, bf16[384,768]{1,0:T(8,128)(2,1)}, u32[]{:S(2)}) copy-start(bf16[384,768]{1,0:T(8,128)(2,1)} %wco_hbm.1) | copy-start | bytes 1769476
  8.4 0.9 %copy-start.6 = (bf16[160,768]{1,0:T(8,128)(2,1)S(1)}, bf16[160,768]{1,0:T(8,128)(2,1)}, u32[]{:S(2)}) copy-start(bf16[160,768]{1,0:T(8,128)(2,1)} %patches_ref.1) | copy-start | bytes 737284

commit v2 on v1

--- a/solution.py
+++ b/solution.py
@@ -54,9 +54,9 @@
 def kernel(
     nx,
     nz,
-    patches_ref,
-    mask_ref,
-    seg_ref,
+    patches_hbm,
+    mask_hbm,
+    seg_hbm,
     wq_hbm,
     wk_hbm,
     wv_hbm,
@@ -66,6 +66,9 @@
     wu_hbm,
     wd_hbm,
     out_ref,
+    patches_ref,
+    mask_ref,
+    seg_ref,
     wproj,
     wo,
     wco,
@@ -78,6 +81,7 @@
     qbuf,
     rsout,
     rsin,
+    acc,
     keys,
     attn_out,
     attn_in,
@@ -85,15 +89,17 @@
     cross_in,
     down_out,
     down_in,
-    result,
-    left_result,
-    right_result,
+    edge_hidden,
+    left_hidden,
+    right_hidden,
+    left_down,
+    right_down,
     wsem,
     ssem,
     rsem,
 ):
     ntm = nx * nz * 4
-    rows_dev, width = patches_ref.shape
+    rows_dev, width = patches_hbm.shape
     half = wq_hbm.shape[1]
     me = lax.axis_index("tm")
     mp = lax.axis_index("mp")
@@ -101,14 +107,29 @@
     yh = lax.rem(me // 2, 2)
     z = lax.rem(me // 4, nz)
     x = me // (4 * nz)
-    sibling = me + 1 - 2 * core
+    sibling = (me + 1 - 2 * core, mp)
     ypart = me + 2 - 4 * yh
     right = lax.rem(me + 1, ntm)
     left = lax.rem(me + ntm - 1, ntm)
-    zpeer = [me + 4 * (lax.rem(z + k, nz) - z) for k in range(nz)]
-    xpeer = [me + 4 * nz * (lax.rem(x + k, nx) - x) for k in range(nx)]
-
-    weights = [
+    right_side = (right, mp + core * (1 - 2 * mp))
+    left_side = (left, mp + (1 - core) * (1 - 2 * mp))
+    partner = (me, 1 - mp)
+    zpeer = [(me + 4 * (lax.rem(z + k, nz) - z), mp) for k in range(nz)]
+    xpeer = [(me + 4 * nz * (lax.rem(x + k, nx) - x), mp) for k in range(nx)]
+    xypeer = [(ypart + 4 * nz * (lax.rem(x + k, nx) - x), mp) for k in range(nx)]
+    neighbours = [(right, mp), (right, 1 - mp), (left, mp), (left, 1 - mp)]
+
+    barrier = pltpu.get_barrier_semaphore()
+    greeted = [sibling, partner] + neighbours + zpeer[1:] + xpeer[1:] + xypeer
+    for target in greeted:
+        pl.semaphore_signal(
+            barrier, inc=1, device_id=target, device_id_type=pl.DeviceIdType.MESH
+        )
+
+    sources = [
+        (mask_hbm, mask_ref),
+        (patches_hbm, patches_ref),
+        (seg_hbm, seg_ref),
         (wq_hbm, wproj.at[:, 0:half]),
         (wk_hbm, wproj.at[:, half : 2 * half]),
         (wv_hbm, wproj.at[:, 2 * half : 3 * half]),
@@ -119,18 +140,10 @@
         (wd_hbm, wd),
     ]
     loads = []
-    for i, (source, target) in enumerate(weights):
+    for i, (source, target) in enumerate(sources):
         load = pltpu.make_async_copy(source, target, wsem.at[i])
         load.start()
         loads.append(load)
-
-    barrier = pltpu.get_barrier_semaphore()
-    greeted = [(sibling, mp), (ypart, mp), (right, mp), (left, mp), (me, 1 - mp)]
-    greeted += [(peer, mp) for peer in zpeer[1:]] + [(peer, mp) for peer in xpeer[1:]]
-    for target in greeted:
-        pl.semaphore_signal(
-            barrier, inc=1, device_id=target, device_id_type=pl.DeviceIdType.MESH
-        )
 
     counter = [0]
     started = []
@@ -150,16 +163,25 @@
         started.append(copy)
         return copy
 
+    loads[0].wait()
     mask = mask_ref[...].astype(F32)
-    before = jnp.where(iota(mask.shape, 0) < me, mask, 0.0)
+    place = iota(mask.shape, 0) * 128 + iota(mask.shape, 1)
+    before = jnp.where(place < me * rows_dev, mask, 0.0)
     base = jnp.sum(jnp.sum(before, axis=1, keepdims=True), axis=0, keepdims=True)
     base = base - (KEPT * me).astype(F32)
-    own_mask = mask_ref[pl.ds(me, 1), :].astype(F32)
-    left_mask = jnp.where(me > 0, mask_ref[pl.ds(left, 1), :].astype(F32), 0.0)
-    right_mask = jnp.where(me < ntm - 1, mask_ref[pl.ds(right, 1), :].astype(F32), 0.0)
-    own_seg = seg_ref[pl.ds(me, 1), :].astype(F32) + 1.0
-    left_seg = seg_ref[pl.ds(left, 1), :].astype(F32) + 1.0
-    right_seg = seg_ref[pl.ds(right, 1), :].astype(F32) + 1.0
+
+    def run_of(ref, index):
+        first = index * rows_dev // 128
+        both = jnp.concatenate([ref[pl.ds(first, 1), :], ref[pl.ds(first + 1, 1), :]], axis=1)
+        phase = lax.rem(index, 4)
+        row = both[:, 0:rows_dev]
+        for k in range(1, 4):
+            row = jnp.where(phase == k, both[:, 32 * k : 32 * k + rows_dev], row)
+        return row.astype(F32)
+
+    own_mask = run_of(mask_ref, me)
+    left_mask = jnp.where(me > 0, run_of(mask_ref, left), 0.0)
+    right_mask = jnp.where(me < ntm - 1, run_of(mask_ref, right), 0.0)
     earlier = (iota((rows_dev, rows_dev), 0) < iota((rows_dev, rows_dev), 1)).astype(F32)
     earlier = earlier.astype(BF16)
 
@@ -170,16 +192,21 @@
         return jnp.where(grid == slot, 1.0, 0.0).astype(BF16)
 
     own_place = window(own_mask, base)
+    loads[1].wait()
     patches = patches_ref[...]
     xwin[...] = dot(own_place, patches).astype(BF16)
 
     pl.semaphore_wait(barrier, len(greeted))
 
-    edge_right = send(
-        xwin.at[WINDOW - EDGE : WINDOW], lwin.at[WINDOW - EDGE : WINDOW], (right, mp)
-    )
-    edge_left = send(xwin.at[0:EDGE], rwin.at[0:EDGE], (left, mp))
-
+    edge_right = send(xwin.at[KEPT + EDGE : WINDOW], lwin.at[KEPT + EDGE : WINDOW], right_side)
+    edge_left = send(xwin.at[0:EDGE], rwin.at[0:EDGE], left_side)
+    halo_right = send(xwin.at[0 : KEPT + EDGE], lwin.at[0 : KEPT + EDGE], right_side)
+    halo_left = send(xwin.at[EDGE:WINDOW], rwin.at[EDGE:WINDOW], left_side)
+
+    loads[2].wait()
+    own_seg = run_of(seg_ref, me) + 1.0
+    left_seg = run_of(seg_ref, left) + 1.0
+    right_seg = run_of(seg_ref, right) + 1.0
     own_count = jnp.sum(own_mask, axis=1, keepdims=True)
     left_count = jnp.sum(left_mask, axis=1, keepdims=True)
     left_place = window(left_mask, base - left_count + float(KEPT))
@@ -221,7 +248,7 @@
         ],
         axis=0,
     )
-    for load in loads[:3]:
+    for load in loads[3:6]:
         load.wait()
     qkv = dot(norm_rows(kept).astype(BF16), wproj[:, : 3 * half])
     qbuf[0:KEPT] = (qkv[:, :half].astype(BF16).astype(F32) * 0.125).astype(BF16)
@@ -230,26 +257,26 @@
     def slots(ref, first, count):
         return ref.at[first * KEPT : (first + count) * KEPT]
 
-    kv_y = send(slots(kvbuf, 0, 1), slots(kvbuf, nx, 1), (ypart, mp))
-    kv_x = [
-        send(slots(kvbuf, 0, 1), slots(kvbuf, nx - k, 1), (xpeer[k], mp)) for k in range(1, nx)
-    ]
+    own_kv, own_q = slots(kvbuf, 0, 1), slots(qbuf, 0, 1)
     far_first = sorted(range(1, nz), key=lambda k: -min(k, nz - k))
-    q_z = [send(slots(qbuf, 0, 1), slots(qbuf, nz - k, 1), (zpeer[k], mp)) for k in far_first]
-    kv_s = [send(slots(kvbuf, 0, 1), slots(kvbuf, 2 * nx, 1), (sibling, mp))]
-    halo_right = send(xwin.at[0 : WINDOW - EDGE], lwin.at[0 : WINDOW - EDGE], (right, mp))
-    halo_left = send(xwin.at[EDGE:WINDOW], rwin.at[EDGE:WINDOW], (left, mp))
-
-    loads[3].wait()
+    far_x = sorted(range(nx), key=lambda k: -min(k, nx - k))
+    q_z, kv_x, kv_xy, kv_s = [], [], [], []
+    for n in range(max(nx, nz)):
+        if n < nx:
+            k = far_x[n]
+            kv_xy.append(send(own_kv, slots(kvbuf, nx + (nx - k) % nx, 1), xypeer[k]))
+        if n < nz - 1:
+            k = far_first[n]
+            q_z.append(send(own_q, slots(qbuf, nz - k, 1), zpeer[k]))
+        if n < nx - 1:
+            k = far_x[n]
+            kv_x.append(send(own_kv, slots(kvbuf, nx - k, 1), xpeer[k]))
+    kv_s.append(send(own_kv, slots(kvbuf, 2 * nx, 1), sibling))
+
+    loads[6].wait()
     own_proj = dot(normed, wproj[:, half:])
     keys[0:rows_dev] = own_proj[:, : 2 * half].astype(BF16)
     cross_query = (own_proj[:, 2 * half :].astype(BF16).astype(F32) * 0.125).astype(BF16)
-
-    kv_y.wait_recv()
-    kv_x2 = [
-        send(slots(kvbuf, nx, 1), slots(kvbuf, 2 * nx - k, 1), (xpeer[k], mp))
-        for k in range(1, nx)
-    ]
 
     halo_right.wait_recv()
     halo_left.wait_recv()
@@ -272,32 +299,28 @@
     npairs = half // 128
     for i in range(npairs):
         cross_pair(i)
-        if i == 0:
-            for copy in kv_x:
-                copy.wait_recv()
-            kv_s.append(send(slots(kvbuf, 1, nx - 1), slots(kvbuf, 2 * nx + 1, nx - 1), (sibling, mp)))
-        if i == 1:
-            for copy in kv_x2:
-                copy.wait_recv()
-            kv_s.append(send(slots(kvbuf, nx, nx), slots(kvbuf, 3 * nx, nx), (sibling, mp)))
-    loads[4].wait()
+    loads[7].wait()
     cross_out[...] = dot(jnp.concatenate(pairs, axis=1), wco[...]).astype(BF16)
-    cross_move = send(cross_out, cross_in, (me, 1 - mp))
-
+
+    for copy in kv_x:
+        copy.wait_recv()
+    kv_s.append(send(slots(kvbuf, 1, nx - 1), slots(kvbuf, 2 * nx + 1, nx - 1), sibling))
+    for copy in kv_xy:
+        copy.wait_recv()
+    kv_s.append(send(slots(kvbuf, nx, nx), slots(kvbuf, 3 * nx, nx), sibling))
+    cross_move = send(cross_out, cross_in, partner)
     for copy in q_z:
         copy.wait_recv()
-    for copy in kv_s:
-        copy.wait_recv()
 
     half_mod = lax.rem(iota((1, 128), 1), 64)
 
-    def partials(queries):
+    def partials(queries, first, last):
         parts, dens = [], []
         for i in range(npairs):
             numerator, denominator = attend_pair(
                 queries[:, 128 * i : 128 * (i + 1)],
-                kvbuf[:, 128 * i : 128 * (i + 1)],
-                kvbuf[:, half + 128 * i : half + 128 * (i + 1)],
+                kvbuf[first:last, 128 * i : 128 * (i + 1)],
+                kvbuf[first:last, half + 128 * i : half + 128 * (i + 1)],
                 None,
             )
             parts.append(numerator)
@@ -307,22 +330,27 @@
             packed = jnp.where(half_mod >= 16 * i, dens[i], packed)
         return jnp.concatenate(parts + [packed], axis=1)
 
+    nkv = kvbuf.shape[0]
+    acc[...] = partials(qbuf[...], 0, nkv // 2)
+    for copy in kv_s:
+        copy.wait_recv()
     rs_move = []
-    quarter = nz // 4
-    far = partials(qbuf[quarter * KEPT : (nz - quarter) * KEPT])
-    rsout[quarter * KEPT : (nz - quarter) * KEPT] = far.astype(BF16)
+    near_far = nz // 4 * KEPT
+    last = nz * KEPT - near_far
+    far = acc[near_far:last] + partials(qbuf[near_far:last], nkv // 2, nkv)
+    rsout[near_far:last] = far.astype(BF16)
     for k in far_first:
-        if quarter <= k < nz - quarter:
-            rs_move.append(send(slots(rsout, k, 1), slots(rsin, nz - k, 1), (zpeer[k], mp)))
+        if near_far <= k * KEPT < last:
+            rs_move.append(send(slots(rsout, k, 1), slots(rsin, nz - k, 1), zpeer[k]))
     close = partials(
-        jnp.concatenate([qbuf[(nz - quarter) * KEPT : nz * KEPT], qbuf[0 : quarter * KEPT]], axis=0)
-    )
-    rsout[(nz - quarter) * KEPT : nz * KEPT] = close[: quarter * KEPT].astype(BF16)
-    rsout[0 : quarter * KEPT] = close[quarter * KEPT :].astype(BF16)
+        jnp.concatenate([qbuf[last:], qbuf[:near_far]], axis=0), nkv // 2, nkv
+    ) + jnp.concatenate([acc[last:], acc[:near_far]], axis=0)
+    rsout[last:] = close[:near_far].astype(BF16)
+    rsout[:near_far] = close[near_far:].astype(BF16)
     for k in far_first:
-        if not quarter <= k < nz - quarter:
-            rs_move.append(send(slots(rsout, k, 1), slots(rsin, nz - k, 1), (zpeer[k], mp)))
-    total = close[quarter * KEPT : (quarter + 1) * KEPT]
+        if not near_far <= k * KEPT < last:
+            rs_move.append(send(slots(rsout, k, 1), slots(rsin, nz - k, 1), zpeer[k]))
+    total = close[near_far : near_far + KEPT]
 
     cross_move.wait_recv()
     pruned = patches.astype(F32) + (cross_out[...].astype(F32) + cross_in[...].astype(F32))
@@ -339,24 +367,45 @@
         attention.append(
             (total[:, 128 * i : 128 * (i + 1)] / jnp.where(low, first, second)).astype(BF16)
         )
-    loads[5].wait()
+    loads[8].wait()
     attn_out[...] = dot(jnp.concatenate(attention, axis=1), wo[...]).astype(BF16)
-    attn_move = send(attn_out, attn_in, (me, 1 - mp))
-    loads[6].wait()
-    loads[7].wait()
+    attn_move = send(attn_out, attn_in, partner)
+    loads[9].wait()
+    loads[10].wait()
     attn_move.wait_recv()
     hidden = kept + (attn_out[...].astype(F32) + attn_in[...].astype(F32))
+    edge_hidden[0:EDGE] = hidden[:EDGE]
+    edge_hidden[EDGE : 2 * EDGE] = hidden[KEPT - EDGE :]
+    hidden_right = send(edge_hidden.at[EDGE : 2 * EDGE], left_hidden, right_side)
+    hidden_left = send(edge_hidden.at[0:EDGE], right_hidden, left_side)
     gated = jax.nn.gelu(dot(norm_rows(hidden).astype(BF16), wu[...]), approximate=True)
     down_out[...] = dot(gated.astype(BF16), wd[...]).astype(BF16)
-    down_move = send(down_out, down_in, (me, 1 - mp))
+    ends = []
+    for n, side in enumerate((mp, 1 - mp)):
+        there = slice(n * EDGE, (n + 1) * EDGE)
+        ends.append(send(down_out.at[KEPT - EDGE : KEPT], left_down.at[there], (right, side)))
+        ends.append(send(down_out.at[0:EDGE], right_down.at[there], (left, side)))
+    down_move = send(down_out, down_in, partner)
+    hidden_right.wait_recv()
+    hidden_left.wait_recv()
     down_move.wait_recv()
-    result[...] = (hidden + (down_out[...].astype(F32) + down_in[...].astype(F32))).astype(BF16)
-    result_right = send(result.at[KEPT - EDGE : KEPT], left_result, (right, mp))
-    result_left = send(result.at[0:EDGE], right_result, (left, mp))
-    result_right.wait_recv()
-    result_left.wait_recv()
-    finished = jnp.concatenate([left_result[...], result[...], right_result[...]], axis=0)
-    spread = dot_0(own_place, finished)
+    own_result = hidden + (down_out[...].astype(F32) + down_in[...].astype(F32))
+    for copy in ends:
+        copy.wait_recv()
+
+    def edge_result(base_ref, parts_ref):
+        parts = parts_ref[...].astype(F32)
+        return base_ref[...] + (parts[:EDGE] + parts[EDGE:])
+
+    finished = jnp.concatenate(
+        [
+            edge_result(left_hidden, left_down),
+            own_result,
+            edge_result(right_hidden, right_down),
+        ],
+        axis=0,
+    )
+    spread = dot_0(own_place, finished.astype(BF16))
     out_ref[...] = jnp.where(kept_column, spread, pruned).astype(BF16)
 
     for copy in started:
@@ -368,15 +417,17 @@
     half = weights[0].shape[1]
     hidden = weights[6].shape[1]
     ntm = nx * nz * 4
-    copies = 24 + 3 * (nx - 1) + 2 * (nz - 1)
+    copies = 17 + 2 * nx + 2 * (nz - 1)
     vmem = lambda *shape: pltpu.VMEM(shape, BF16)
     return pl.pallas_call(
         functools.partial(kernel, nx, nz),
         out_shape=jax.ShapeDtypeStruct((rows, width), BF16),
-        in_specs=[pl.BlockSpec(memory_space=pltpu.VMEM)] * 3
-        + [pl.BlockSpec(memory_space=pl.ANY)] * 8,
+        in_specs=[pl.BlockSpec(memory_space=pl.ANY)] * 11,
         out_specs=pl.BlockSpec(memory_space=pltpu.VMEM),
         scratch_shapes=[
+            vmem(rows, width),
+            pltpu.VMEM((ntm * rows // 128, 128), jnp.int32),
+            pltpu.VMEM((ntm * rows // 128, 128), jnp.int32),
             vmem(width, 4 * half),
             vmem(half, width),
             vmem(half, width),
@@ -389,6 +440,7 @@
             vmem(nz * KEPT, half),
             vmem(nz * KEPT, half + 128),
             vmem(nz * KEPT, half + 128),
+            pltpu.VMEM((nz * KEPT, half + 128), F32),
             vmem(rows + 2 * WINDOW, 2 * half),
             vmem(KEPT, width),
             vmem(KEPT, width),
@@ -396,17 +448,19 @@
             vmem(rows, width),
             vmem(KEPT, width),
             vmem(KEPT, width),
-            vmem(KEPT, width),
-            vmem(EDGE, width),
-            vmem(EDGE, width),
-            pltpu.SemaphoreType.DMA((8,)),
+            pltpu.VMEM((2 * EDGE, width), F32),
+            pltpu.VMEM((EDGE, width), F32),
+            pltpu.VMEM((EDGE, width), F32),
+            vmem(2 * EDGE, width),
+            vmem(2 * EDGE, width),
+            pltpu.SemaphoreType.DMA((11,)),
             pltpu.SemaphoreType.DMA((copies,)),
             pltpu.SemaphoreType.DMA((copies,)),
         ],
         compiler_params=pltpu.CompilerParams(
-            collective_id=0, has_side_effects=True, vmem_limit_bytes=48 * 1024 * 1024
+            collective_id=0, has_side_effects=True, vmem_limit_bytes=60 * 1024 * 1024
         ),
-    )(patches, keep_mask.reshape(ntm, rows), segment.reshape(ntm, rows), *weights)
+    )(patches, keep_mask.reshape(-1, 128), segment.reshape(-1, 128), *weights)
 
 
 def solution(mesh):

time: 63.3 us -> 48.5 us (0.77)
  local copies, waits for them, and re-layouts: 9.98 us -> 1.65 us
  Pallas kernels: 52.8 us -> 46.7 us
    unnamed x15 -> x1, local copies, waits for them, and re-layouts: 8.02 us -> 1.65 us
    pallas_call x1, Pallas kernels: 52.8 us -> 46.7 us  [body(): pl.pallas_call(functools.partial(kernel, nx, nz), out_shape=jax.ShapeDtyp...]
    reshape x2 -> x0, local copies, waits for them, and re-layouts: 1.97 us -> none  [the longest x1 0.99 us: body(): segment.reshape(ntm, rows)]
where the time goes in v2:
time: 48.5 us; the launch traced here: 48.4 us
  Pallas kernels  46.7 us (96%)
  local copies, waits for them, and re-layouts  1.65 us (3%)
    pallas_call x1, Pallas kernels, body(): pl.pallas_call(functools.partial(kernel, nx, nz), out_shape=jax.ShapeDtyp...  46.7 us
    unnamed x1, local copies, waits for them, and re-layouts  1.65 us

profile of v2, /device:TPU:1, one launch (start us, length us, event | category | flops | bytes accessed | tf_op | source)
XLA Modules:
  0.0 48.4 jit_solution(14398014934746541232)
XLA Ops:
  0.0 46.7 %shard_map.109 = bf16[160,768]{1,0:T(8,128)(2,1)} custom-call(bf16[160,768]{1,0:T(8,128)(2,1)} %patches_hbm.1, s32[160,128]{1,0:T(8,128)} %bitcast.2, s32[160,128]{1,0:T(8,128)} %bitcast.3, bf16[768,384]{1,0:T(8,128)(2,1)} %wq_hbm.1, bf16[768,384]{1,0:T(8,128)(2,1)} %wk_hbm.1, bf16[768,384]{1,0:T(8,128)(2,1)} %wv_hbm.1, bf16[384,768]{1,0:T(8,128)(2,1)} %wo_hbm.1, ...), custom_call_target="tpu_custom_call" | custom-call | tf_op jit(solution)/shard_map/pallas_call | solution.py:422
  46.8 1.7 %copy.13 = bf16[160,768]{1,0:T(8,128)(2,1)} copy(bf16[160,768]{1,0:T(8,128)(2,1)} %shard_map.109) | data formatting | bytes 491520

commit v3 on v2

--- a/solution.py
+++ b/solution.py
@@ -81,7 +81,6 @@
     qbuf,
     rsout,
     rsin,
-    acc,
     keys,
     attn_out,
     attn_in,
@@ -251,27 +250,41 @@
     for load in loads[3:6]:
         load.wait()
     qkv = dot(norm_rows(kept).astype(BF16), wproj[:, : 3 * half])
-    qbuf[0:KEPT] = (qkv[:, :half].astype(BF16).astype(F32) * 0.125).astype(BF16)
-    kvbuf[0:KEPT] = qkv[:, half:].astype(BF16)
-
-    def slots(ref, first, count):
-        return ref.at[first * KEPT : (first + count) * KEPT]
-
-    own_kv, own_q = slots(kvbuf, 0, 1), slots(qbuf, 0, 1)
+    queries = (qkv[:, :half].astype(BF16).astype(F32) * 0.125).astype(BF16)
+    kept_kv = qkv[:, half:].astype(BF16)
+    npairs = half // 128
+    nkv, nq = 4 * nx * KEPT, nz * KEPT
+    for p in range(npairs):
+        lanes = slice(128 * p, 128 * (p + 1))
+        qbuf[p * nq : p * nq + KEPT] = queries[:, lanes]
+        kvbuf[p * nkv : p * nkv + KEPT, :128] = kept_kv[:, :half][:, lanes]
+        kvbuf[p * nkv : p * nkv + KEPT, 128:] = kept_kv[:, half:][:, lanes]
+
+    def kv_slots(p, first, count):
+        return kvbuf.at[p * nkv + first * KEPT : p * nkv + (first + count) * KEPT]
+
+    def q_slot(p, k):
+        return qbuf.at[p * nq + k * KEPT : p * nq + (k + 1) * KEPT]
+
     far_first = sorted(range(1, nz), key=lambda k: -min(k, nz - k))
     far_x = sorted(range(nx), key=lambda k: -min(k, nx - k))
     q_z, kv_x, kv_xy, kv_s = [], [], [], []
-    for n in range(max(nx, nz)):
-        if n < nx:
-            k = far_x[n]
-            kv_xy.append(send(own_kv, slots(kvbuf, nx + (nx - k) % nx, 1), xypeer[k]))
-        if n < nz - 1:
-            k = far_first[n]
-            q_z.append(send(own_q, slots(qbuf, nz - k, 1), zpeer[k]))
-        if n < nx - 1:
-            k = far_x[n]
-            kv_x.append(send(own_kv, slots(kvbuf, nx - k, 1), xpeer[k]))
-    kv_s.append(send(own_kv, slots(kvbuf, 2 * nx, 1), sibling))
+    for p in range(npairs):
+        q_z.append([])
+        kv_x.append([])
+        kv_xy.append([])
+        own_kv = kv_slots(p, 0, 1)
+        for n in range(max(nx, nz)):
+            if n < nx:
+                k = far_x[n]
+                kv_xy[p].append(send(own_kv, kv_slots(p, nx + (nx - k) % nx, 1), xypeer[k]))
+            if n < nz - 1:
+                k = far_first[n]
+                q_z[p].append(send(q_slot(p, 0), q_slot(p, nz - k), zpeer[k]))
+            if n < nx - 1:
+                k = far_x[n]
+                kv_x[p].append(send(own_kv, kv_slots(p, nx - k, 1), xpeer[k]))
+        kv_s.append([send(own_kv, kv_slots(p, 2 * nx, 1), sibling)])
 
     loads[6].wait()
     own_proj = dot(normed, wproj[:, half:])
@@ -296,77 +309,77 @@
         )
         pairs.append((numerator / denominator).astype(BF16))
 
-    npairs = half // 128
     for i in range(npairs):
         cross_pair(i)
     loads[7].wait()
     cross_out[...] = dot(jnp.concatenate(pairs, axis=1), wco[...]).astype(BF16)
 
-    for copy in kv_x:
-        copy.wait_recv()
-    kv_s.append(send(slots(kvbuf, 1, nx - 1), slots(kvbuf, 2 * nx + 1, nx - 1), sibling))
-    for copy in kv_xy:
-        copy.wait_recv()
-    kv_s.append(send(slots(kvbuf, nx, nx), slots(kvbuf, 3 * nx, nx), sibling))
-    cross_move = send(cross_out, cross_in, partner)
-    for copy in q_z:
-        copy.wait_recv()
-
     half_mod = lax.rem(iota((1, 128), 1), 64)
-
-    def partials(queries, first, last):
-        parts, dens = [], []
-        for i in range(npairs):
-            numerator, denominator = attend_pair(
-                queries[:, 128 * i : 128 * (i + 1)],
-                kvbuf[first:last, 128 * i : 128 * (i + 1)],
-                kvbuf[first:last, half + 128 * i : half + 128 * (i + 1)],
-                None,
-            )
-            parts.append(numerator)
-            dens.append(denominator)
-        packed = dens[0]
-        for i in range(1, npairs):
-            packed = jnp.where(half_mod >= 16 * i, dens[i], packed)
-        return jnp.concatenate(parts + [packed], axis=1)
-
-    nkv = kvbuf.shape[0]
-    acc[...] = partials(qbuf[...], 0, nkv // 2)
-    for copy in kv_s:
-        copy.wait_recv()
-    rs_move = []
-    near_far = nz // 4 * KEPT
-    last = nz * KEPT - near_far
-    far = acc[near_far:last] + partials(qbuf[near_far:last], nkv // 2, nkv)
-    rsout[near_far:last] = far.astype(BF16)
-    for k in far_first:
-        if near_far <= k * KEPT < last:
-            rs_move.append(send(slots(rsout, k, 1), slots(rsin, nz - k, 1), zpeer[k]))
-    close = partials(
-        jnp.concatenate([qbuf[last:], qbuf[:near_far]], axis=0), nkv // 2, nkv
-    ) + jnp.concatenate([acc[last:], acc[:near_far]], axis=0)
-    rsout[last:] = close[:near_far].astype(BF16)
-    rsout[:near_far] = close[near_far:].astype(BF16)
-    for k in far_first:
-        if not near_far <= k * KEPT < last:
-            rs_move.append(send(slots(rsout, k, 1), slots(rsin, nz - k, 1), zpeer[k]))
-    total = close[near_far : near_far + KEPT]
+    block = npairs * KEPT + 16
+    head_lane = 64 * lax.rem(iota((16, 128), 0), 2) + 16 * (iota((16, 128), 0) // 2)
+    pick = jnp.where(iota((16, 128), 1) == head_lane, 1.0, 0.0)
+    pick = jnp.where(iota((16, 128), 0) < 2 * npairs, pick, 0.0).astype(BF16)
+    totals, rs_move, packed = [], [], None
+    for p in range(npairs):
+        for copy in kv_x[p]:
+            copy.wait_recv()
+        kv_s[p].append(send(kv_slots(p, 1, nx - 1), kv_slots(p, 2 * nx + 1, nx - 1), sibling))
+        for copy in kv_xy[p]:
+            copy.wait_recv()
+        kv_s[p].append(send(kv_slots(p, nx, nx), kv_slots(p, 3 * nx, nx), sibling))
+        if p == npairs - 1:
+            cross_move = send(cross_out, cross_in, partner)
+        for copy in q_z[p]:
+            copy.wait_recv()
+        ring = qbuf[p * nq : (p + 1) * nq]
+        first = slice(p * nkv, p * nkv + nkv // 2)
+        second = slice(p * nkv + nkv // 2, (p + 1) * nkv)
+        num, den = attend_pair(ring, kvbuf[first, :128], kvbuf[first, 128:], None)
+        for copy in kv_s[p]:
+            copy.wait_recv()
+        num2, den2 = attend_pair(ring, kvbuf[second, :128], kvbuf[second, 128:], None)
+        num, den = num + num2, den + den2
+        packed = den if p == 0 else jnp.where(half_mod >= 16 * p, den, packed)
+        totals.append(num[:KEPT])
+        num = num.astype(BF16)
+        for k in far_first + [0]:
+            rows = slice(k * KEPT, (k + 1) * KEPT)
+            there = k * block + p * KEPT
+            count = KEPT
+            if k:
+                rsout[there : there + KEPT] = num[rows]
+            if p == npairs - 1:
+                own = jnp.concatenate([packed[rows], jnp.zeros((128 - KEPT, 128), F32)], axis=0)
+                by_head = dot_t(pick, own.astype(BF16))
+                count = KEPT + 16
+                if k:
+                    rsout[there + KEPT : there + count] = by_head.astype(BF16)
+                else:
+                    totals.append(by_head)
+            if k:
+                back = (nz - k) * block + p * KEPT
+                rs_move.append(
+                    send(rsout.at[there : there + count], rsin.at[back : back + count], zpeer[k])
+                )
 
     cross_move.wait_recv()
     pruned = patches.astype(F32) + (cross_out[...].astype(F32) + cross_in[...].astype(F32))
 
     for copy in rs_move:
         copy.wait_recv()
-    for k in range(1, nz):
-        total = total + rsin[k * KEPT : (k + 1) * KEPT].astype(F32)
-    low = iota((KEPT, 128), 1) < 64
-    attention = []
-    for i in range(npairs):
-        first = total[:, half + 16 * i : half + 16 * i + 1]
-        second = total[:, half + 64 + 16 * i : half + 64 + 16 * i + 1]
-        attention.append(
-            (total[:, 128 * i : 128 * (i + 1)] / jnp.where(low, first, second)).astype(BF16)
-        )
+    for p in range(npairs + 1):
+        for k in range(1, nz):
+            there = k * block + p * KEPT
+            totals[p] += rsin[there : there + totals[p].shape[0]].astype(F32)
+    by_head = totals[npairs]
+    inverse = jnp.where(by_head > 0.0, 1.0 / by_head, 0.0)
+    coarse = inverse.astype(BF16)
+    fine = (inverse - coarse.astype(F32)).astype(BF16)
+    widen = jnp.where(iota((16, half), 1) // 64 == iota((16, half), 0), 1.0, 0.0).astype(BF16)
+    inverse = (dot_0(coarse, widen) + dot_0(fine, widen))[:KEPT]
+    attention = [
+        (totals[p] * inverse[:, 128 * p : 128 * (p + 1)]).astype(BF16) for p in range(npairs)
+    ]
     loads[8].wait()
     attn_out[...] = dot(jnp.concatenate(attention, axis=1), wo[...]).astype(BF16)
     attn_move = send(attn_out, attn_in, partner)
@@ -417,11 +430,12 @@
     half = weights[0].shape[1]
     hidden = weights[6].shape[1]
     ntm = nx * nz * 4
-    copies = 17 + 2 * nx + 2 * (nz - 1)
+    npairs = half // 128
+    copies = 14 + npairs * (2 * nx + 2 + 2 * (nz - 1))
     vmem = lambda *shape: pltpu.VMEM(shape, BF16)
     return pl.pallas_call(
         functools.partial(kernel, nx, nz),
-        out_shape=jax.ShapeDtypeStruct((rows, width), BF16),
+        out_shape=pltpu.VMEM((rows, width), BF16),
         in_specs=[pl.BlockSpec(memory_space=pl.ANY)] * 11,
         out_specs=pl.BlockSpec(memory_space=pltpu.VMEM),
         scratch_shapes=[
@@ -436,11 +450,10 @@
             vmem(WINDOW, width),
             vmem(WINDOW, width),
             vmem(WINDOW, width),
-            vmem(4 * nx * KEPT, 2 * half),
-            vmem(nz * KEPT, half),
-            vmem(nz * KEPT, half + 128),
-            vmem(nz * KEPT, half + 128),
-            pltpu.VMEM((nz * KEPT, half + 128), F32),
+            vmem(npairs * 4 * nx * KEPT, 256),
+            vmem(npairs * nz * KEPT, 128),
+            vmem(nz * (npairs * KEPT + 16), 128),
+            vmem(nz * (npairs * KEPT + 16), 128),
             vmem(rows + 2 * WINDOW, 2 * half),
             vmem(KEPT, width),
             vmem(KEPT, width),

time: 48.5 us -> 44.9 us (0.926)
  the two profiles are of different devices: /device:TPU:1 before, /device:TPU:10 now
where the time goes in v3:
time: 44.9 us; the launch traced here: 44.8 us
  Pallas kernels  44.1 us (98%)
  local copies, waits for them, and re-layouts  0.7 us (2%)
    pallas_call x1, Pallas kernels, body(): pl.pallas_call(functools.partial(kernel, nx, nz), out_shape=pltpu.VMEM((r...  44.1 us

profile of v3, /device:TPU:10, one launch (start us, length us, event | category | flops | bytes accessed | tf_op | source)
XLA Modules:
  0.0 44.8 jit_solution(320527949633382)
XLA Ops:
  0.0 44.1 %shard_map.109 = bf16[160,768]{1,0:T(8,128)(2,1)S(1)} custom-call(bf16[160,768]{1,0:T(8,128)(2,1)} %patches_hbm.1, s32[160,128]{1,0:T(8,128)} %bitcast.2, s32[160,128]{1,0:T(8,128)} %bitcast.3, bf16[768,384]{1,0:T(8,128)(2,1)} %wq_hbm.1, bf16[768,384]{1,0:T(8,128)(2,1)} %wk_hbm.1, bf16[768,384]{1,0:T(8,128)(2,1)} %wv_hbm.1, bf16[384,768]{1,0:T(8,128)(2,1)} %wo_hbm.1, ...), custom_call_target="tpu_custom_call" | custom-call | tf_op jit(solution)/shard_map/pallas_call | solution.py:436
  44.1 0.7 %copy.13 = bf16[160,768]{1,0:T(8,128)(2,1)} copy(bf16[160,768]{1,0:T(8,128)(2,1)S(1)} %shard_map.109) | data formatting | bytes 491520

commit v4 on v3

--- a/solution.py
+++ b/solution.py
@@ -327,7 +327,7 @@
         for copy in kv_xy[p]:
             copy.wait_recv()
         kv_s[p].append(send(kv_slots(p, nx, nx), kv_slots(p, 3 * nx, nx), sibling))
-        if p == npairs - 1:
+        if p == 0:
             cross_move = send(cross_out, cross_in, partner)
         for copy in q_z[p]:
             copy.wait_recv()
@@ -361,9 +361,6 @@
                 rs_move.append(
                     send(rsout.at[there : there + count], rsin.at[back : back + count], zpeer[k])
                 )
-
-    cross_move.wait_recv()
-    pruned = patches.astype(F32) + (cross_out[...].astype(F32) + cross_in[...].astype(F32))
 
     for copy in rs_move:
         copy.wait_recv()
@@ -409,6 +406,9 @@
     def edge_result(base_ref, parts_ref):
         parts = parts_ref[...].astype(F32)
         return base_ref[...] + (parts[:EDGE] + parts[EDGE:])
+
+    cross_move.wait_recv()
+    pruned = patches.astype(F32) + (cross_out[...].astype(F32) + cross_in[...].astype(F32))
 
     finished = jnp.concatenate(
         [

time: 44.9 us -> 43.9 us (0.978)
  the two profiles are of different devices: /device:TPU:10 before, /device:TPU:1 now
where the time goes in v4:
time: 43.9 us; the launch traced here: 43.8 us
  Pallas kernels  43.1 us (98%)
  local copies, waits for them, and re-layouts  0.7 us (2%)
    pallas_call x1, Pallas kernels, body(): pl.pallas_call(functools.partial(kernel, nx, nz), out_shape=pltpu.VMEM((r...  43.1 us

profile of v4, /device:TPU:1, one launch (start us, length us, event | category | flops | bytes accessed | tf_op | source)
XLA Modules:
  0.0 43.8 jit_solution(12570869965388155253)
XLA Ops:
  0.0 43.1 %shard_map.109 = bf16[160,768]{1,0:T(8,128)(2,1)S(1)} custom-call(bf16[160,768]{1,0:T(8,128)(2,1)} %patches_hbm.1, s32[160,128]{1,0:T(8,128)} %bitcast.2, s32[160,128]{1,0:T(8,128)} %bitcast.3, bf16[768,384]{1,0:T(8,128)(2,1)} %wq_hbm.1, bf16[768,384]{1,0:T(8,128)(2,1)} %wk_hbm.1, bf16[768,384]{1,0:T(8,128)(2,1)} %wv_hbm.1, bf16[384,768]{1,0:T(8,128)(2,1)} %wo_hbm.1, ...), custom_call_target="tpu_custom_call" | custom-call | tf_op jit(solution)/shard_map/pallas_call | solution.py:436
  43.1 0.7 %copy.13 = bf16[160,768]{1,0:T(8,128)(2,1)} copy(bf16[160,768]{1,0:T(8,128)(2,1)S(1)} %shard_map.109) | data formatting | bytes 491520

commit v5 on v4

--- a/solution.py
+++ b/solution.py
@@ -49,6 +49,26 @@
     numerator = jnp.where(low, total[:rows, :128], total[rows:, :128])
     denominator = jnp.where(low, total[:rows, 128:], total[rows:, 128:])
     return numerator, denominator
+
+
+class Move:
+    def __init__(self, copy, going, coming):
+        self.copy, self.going, self.coming = copy, going, coming
+
+    def start(self):
+        self.run(self.going, self.copy.start)
+
+    def wait_recv(self):
+        self.run(self.coming, self.copy.wait_recv)
+
+    def wait_send(self):
+        self.run(self.going, self.copy.wait_send)
+
+    def run(self, condition, step):
+        if condition is None:
+            step()
+        else:
+            pl.when(condition)(lambda: step())
 
 
 def kernel(
@@ -116,14 +136,21 @@
     zpeer = [(me + 4 * (lax.rem(z + k, nz) - z), mp) for k in range(nz)]
     xpeer = [(me + 4 * nz * (lax.rem(x + k, nx) - x), mp) for k in range(nx)]
     xypeer = [(ypart + 4 * nz * (lax.rem(x + k, nx) - x), mp) for k in range(nx)]
-    neighbours = [(right, mp), (right, 1 - mp), (left, mp), (left, 1 - mp)]
+    has_left, has_right = me > 0, me < ntm - 1
 
     barrier = pltpu.get_barrier_semaphore()
-    greeted = [sibling, partner] + neighbours + zpeer[1:] + xpeer[1:] + xypeer
-    for target in greeted:
-        pl.semaphore_signal(
-            barrier, inc=1, device_id=target, device_id_type=pl.DeviceIdType.MESH
-        )
+
+    def greet(targets):
+        for target in targets:
+            pl.semaphore_signal(
+                barrier, inc=1, device_id=target, device_id_type=pl.DeviceIdType.MESH
+            )
+
+    fixed = [sibling, partner] + zpeer[1:] + xpeer[1:] + xypeer
+    greet(fixed)
+    pl.when(has_left)(lambda: greet([(left, mp), (left, 1 - mp)]))
+    pl.when(has_right)(lambda: greet([(right, mp), (right, 1 - mp)]))
+    greeted = len(fixed) + 2 * jnp.minimum(me, 1) + 2 * jnp.minimum(ntm - 1 - me, 1)
 
     sources = [
         (mask_hbm, mask_ref),
@@ -147,7 +174,7 @@
     counter = [0]
     started = []
 
-    def send(source, target, where):
+    def send(source, target, where, going=None, coming=None):
         i = counter[0]
         counter[0] += 1
         copy = pltpu.make_async_remote_copy(
@@ -158,9 +185,16 @@
             device_id=where,
             device_id_type=pl.DeviceIdType.MESH,
         )
-        copy.start()
-        started.append(copy)
-        return copy
+        move = Move(copy, going, coming)
+        move.start()
+        started.append(move)
+        return move
+
+    def send_right(source, target, where):
+        return send(source, target, where, has_right, has_left)
+
+    def send_left(source, target, where):
+        return send(source, target, where, has_left, has_right)
 
     loads[0].wait()
     mask = mask_ref[...].astype(F32)
@@ -195,12 +229,19 @@
     patches = patches_ref[...]
     xwin[...] = dot(own_place, patches).astype(BF16)
 
-    pl.semaphore_wait(barrier, len(greeted))
-
-    edge_right = send(xwin.at[KEPT + EDGE : WINDOW], lwin.at[KEPT + EDGE : WINDOW], right_side)
-    edge_left = send(xwin.at[0:EDGE], rwin.at[0:EDGE], left_side)
-    halo_right = send(xwin.at[0 : KEPT + EDGE], lwin.at[0 : KEPT + EDGE], right_side)
-    halo_left = send(xwin.at[EDGE:WINDOW], rwin.at[EDGE:WINDOW], left_side)
+    def clear(*refs):
+        for ref in refs:
+            ref[...] = jnp.zeros(ref.shape, ref.dtype)
+
+    pl.when(me == 0)(lambda: clear(lwin, left_hidden, left_down))
+    pl.when(me == ntm - 1)(lambda: clear(rwin, right_hidden, right_down))
+
+    pl.semaphore_wait(barrier, greeted)
+
+    edge_right = send_right(xwin.at[KEPT + EDGE : WINDOW], lwin.at[KEPT + EDGE : WINDOW], right_side)
+    edge_left = send_left(xwin.at[0:EDGE], rwin.at[0:EDGE], left_side)
+    halo_right = send_right(xwin.at[0 : KEPT + EDGE], lwin.at[0 : KEPT + EDGE], right_side)
+    halo_left = send_left(xwin.at[EDGE:WINDOW], rwin.at[EDGE:WINDOW], left_side)
 
     loads[2].wait()
     own_seg = run_of(seg_ref, me) + 1.0
@@ -241,9 +282,9 @@
     kept = jnp.concatenate(
         [
             own_rows[:EDGE]
-            + jnp.where(me > 0, lwin[WINDOW - EDGE : WINDOW].astype(F32), 0.0),
+            + lwin[WINDOW - EDGE : WINDOW].astype(F32),
             own_rows[EDGE : KEPT - EDGE],
-            own_rows[KEPT - EDGE :] + jnp.where(me < ntm - 1, rwin[0:EDGE].astype(F32), 0.0),
+            own_rows[KEPT - EDGE :] + rwin[0:EDGE].astype(F32),
         ],
         axis=0,
     )
@@ -362,9 +403,9 @@
                     send(rsout.at[there : there + count], rsin.at[back : back + count], zpeer[k])
                 )
 
-    for copy in rs_move:
-        copy.wait_recv()
     for p in range(npairs + 1):
+        for copy in rs_move[p * (nz - 1) : (p + 1) * (nz - 1)]:
+            copy.wait_recv()
         for k in range(1, nz):
             there = k * block + p * KEPT
             totals[p] += rsin[there : there + totals[p].shape[0]].astype(F32)
@@ -386,15 +427,15 @@
     hidden = kept + (attn_out[...].astype(F32) + attn_in[...].astype(F32))
     edge_hidden[0:EDGE] = hidden[:EDGE]
     edge_hidden[EDGE : 2 * EDGE] = hidden[KEPT - EDGE :]
-    hidden_right = send(edge_hidden.at[EDGE : 2 * EDGE], left_hidden, right_side)
-    hidden_left = send(edge_hidden.at[0:EDGE], right_hidden, left_side)
+    hidden_right = send_right(edge_hidden.at[EDGE : 2 * EDGE], left_hidden, right_side)
+    hidden_left = send_left(edge_hidden.at[0:EDGE], right_hidden, left_side)
     gated = jax.nn.gelu(dot(norm_rows(hidden).astype(BF16), wu[...]), approximate=True)
     down_out[...] = dot(gated.astype(BF16), wd[...]).astype(BF16)
     ends = []
     for n, side in enumerate((mp, 1 - mp)):
         there = slice(n * EDGE, (n + 1) * EDGE)
-        ends.append(send(down_out.at[KEPT - EDGE : KEPT], left_down.at[there], (right, side)))
-        ends.append(send(down_out.at[0:EDGE], right_down.at[there], (left, side)))
+        ends.append(send_right(down_out.at[KEPT - EDGE : KEPT], left_down.at[there], (right, side)))
+        ends.append(send_left(down_out.at[0:EDGE], right_down.at[there], (left, side)))
     down_move = send(down_out, down_in, partner)
     hidden_right.wait_recv()
     hidden_left.wait_recv()

time: 43.9 us -> 43.6 us (level)
  no operation moved by 1% of the time
where the time goes in v5:
time: 43.6 us
  Pallas kernels  42.9 us (98%)
  local copies, waits for them, and re-layouts  0.7 us (2%)
    pallas_call x1, Pallas kernels, body(): pl.pallas_call(functools.partial(kernel, nx, nz), out_shape=pltpu.VMEM((r...  42.9 us

profile of v5, /device:TPU:1, one launch (start us, length us, event | category | flops | bytes accessed | tf_op | source)
XLA Modules:
  0.0 43.6 jit_solution(4083049858797547233)
XLA Ops:
  0.0 42.9 %shard_map.109 = bf16[160,768]{1,0:T(8,128)(2,1)S(1)} custom-call(bf16[160,768]{1,0:T(8,128)(2,1)} %patches_hbm.1, s32[160,128]{1,0:T(8,128)} %bitcast.2, s32[160,128]{1,0:T(8,128)} %bitcast.3, bf16[768,384]{1,0:T(8,128)(2,1)} %wq_hbm.1, bf16[768,384]{1,0:T(8,128)(2,1)} %wk_hbm.1, bf16[768,384]{1,0:T(8,128)(2,1)} %wv_hbm.1, bf16[384,768]{1,0:T(8,128)(2,1)} %wo_hbm.1, ...), custom_call_target="tpu_custom_call" | custom-call | tf_op jit(solution)/shard_map/pallas_call | solution.py:477
  42.9 0.7 %copy.13 = bf16[160,768]{1,0:T(8,128)(2,1)} copy(bf16[160,768]{1,0:T(8,128)(2,1)S(1)} %shard_map.109) | data formatting | bytes 491520

commit v6 on v5

--- a/solution.py
+++ b/solution.py
@@ -156,9 +156,15 @@
         (mask_hbm, mask_ref),
         (patches_hbm, patches_ref),
         (seg_hbm, seg_ref),
-        (wq_hbm, wproj.at[:, 0:half]),
-        (wk_hbm, wproj.at[:, half : 2 * half]),
-        (wv_hbm, wproj.at[:, 2 * half : 3 * half]),
+    ]
+    npairs = half // 128
+    for p in range(npairs):
+        for n, weight in enumerate((wq_hbm, wk_hbm, wv_hbm)):
+            there = (3 * p + n) * 128
+            sources.append(
+                (weight.at[:, 128 * p : 128 * (p + 1)], wproj.at[:, there : there + 128])
+            )
+    sources += [
         (wcq_hbm, wproj.at[:, 3 * half : 4 * half]),
         (wco_hbm, wco),
         (wo_hbm, wo),
@@ -170,6 +176,9 @@
         load = pltpu.make_async_copy(source, target, wsem.at[i])
         load.start()
         loads.append(load)
+
+    pair_loads = loads[3 : 3 + 3 * npairs]
+    loads = loads[:3] + [None] * 3 + loads[3 + 3 * npairs :]
 
     counter = [0]
     started = []
@@ -288,18 +297,8 @@
         ],
         axis=0,
     )
-    for load in loads[3:6]:
-        load.wait()
-    qkv = dot(norm_rows(kept).astype(BF16), wproj[:, : 3 * half])
-    queries = (qkv[:, :half].astype(BF16).astype(F32) * 0.125).astype(BF16)
-    kept_kv = qkv[:, half:].astype(BF16)
-    npairs = half // 128
     nkv, nq = 4 * nx * KEPT, nz * KEPT
-    for p in range(npairs):
-        lanes = slice(128 * p, 128 * (p + 1))
-        qbuf[p * nq : p * nq + KEPT] = queries[:, lanes]
-        kvbuf[p * nkv : p * nkv + KEPT, :128] = kept_kv[:, :half][:, lanes]
-        kvbuf[p * nkv : p * nkv + KEPT, 128:] = kept_kv[:, half:][:, lanes]
+    normed_kept = norm_rows(kept).astype(BF16)
 
     def kv_slots(p, first, count):
         return kvbuf.at[p * nkv + first * KEPT : p * nkv + (first + count) * KEPT]
@@ -314,6 +313,12 @@
         q_z.append([])
         kv_x.append([])
         kv_xy.append([])
+        for load in pair_loads[3 * p : 3 * (p + 1)]:
+            load.wait()
+        qkv = dot(normed_kept, wproj[:, 384 * p : 384 * (p + 1)])
+        queries = qkv[:, :128].astype(BF16).astype(F32) * 0.125
+        qbuf[p * nq : p * nq + KEPT] = queries.astype(BF16)
+        kvbuf[p * nkv : p * nkv + KEPT] = qkv[:, 128:].astype(BF16)
         own_kv = kv_slots(p, 0, 1)
         for n in range(max(nx, nz)):
             if n < nx:
@@ -328,24 +333,28 @@
         kv_s.append([send(own_kv, kv_slots(p, 2 * nx, 1), sibling)])
 
     loads[6].wait()
-    own_proj = dot(normed, wproj[:, half:])
-    keys[0:rows_dev] = own_proj[:, : 2 * half].astype(BF16)
-    cross_query = (own_proj[:, 2 * half :].astype(BF16).astype(F32) * 0.125).astype(BF16)
+    cross_query = dot(normed, wproj[:, 3 * half :]).astype(BF16).astype(F32) * 0.125
+    cross_query = cross_query.astype(BF16)
+
+    def project_keys(rows, first, last):
+        for p in range(npairs):
+            columns = wproj[:, 384 * p + 128 : 384 * (p + 1)]
+            keys[first:last, 256 * p : 256 * (p + 1)] = dot(rows, columns).astype(BF16)
+
+    project_keys(normed, 0, rows_dev)
 
     halo_right.wait_recv()
     halo_left.wait_recv()
     near = jnp.concatenate([lwin[...], rwin[...]], axis=0)
-    keys[rows_dev:nkeys] = dot(
-        norm_rows(near).astype(BF16), wproj[:, half : 3 * half]
-    ).astype(BF16)
+    project_keys(norm_rows(near).astype(BF16), rows_dev, nkeys)
 
     pairs = []
 
     def cross_pair(i):
         numerator, denominator = attend_pair(
             cross_query[:, 128 * i : 128 * (i + 1)],
-            keys[:, 128 * i : 128 * (i + 1)],
-            keys[:, half + 128 * i : half + 128 * (i + 1)],
+            keys[:, 256 * i : 256 * i + 128],
+            keys[:, 256 * i + 128 : 256 * (i + 1)],
             usable,
         )
         pairs.append((numerator / denominator).astype(BF16))
@@ -507,7 +516,7 @@
             pltpu.VMEM((EDGE, width), F32),
             vmem(2 * EDGE, width),
             vmem(2 * EDGE, width),
-            pltpu.SemaphoreType.DMA((11,)),
+            pltpu.SemaphoreType.DMA((8 + 3 * npairs,)),
             pltpu.SemaphoreType.DMA((copies,)),
             pltpu.SemaphoreType.DMA((copies,)),
         ],

time: 43.6 us -> 44.9 us (1.030)
  the two profiles are of different devices: /device:TPU:1 before, /device:TPU:6 now
where the time goes in v6:
time: 44.9 us
  Pallas kernels  44.2 us (98%)
  local copies, waits for them, and re-layouts  0.7 us (2%)
    pallas_call x1, Pallas kernels, body(): pl.pallas_call(functools.partial(kernel, nx, nz), out_shape=pltpu.VMEM((r...  44.2 us

profile of v6, /device:TPU:6, one launch (start us, length us, event | category | flops | bytes accessed | tf_op | source)
XLA Modules:
  0.0 44.9 jit_solution(17989775166756003813)
XLA Ops:
  0.0 44.2 %shard_map.109 = bf16[160,768]{1,0:T(8,128)(2,1)S(1)} custom-call(bf16[160,768]{1,0:T(8,128)(2,1)} %patches_hbm.1, s32[160,128]{1,0:T(8,128)} %bitcast.2, s32[160,128]{1,0:T(8,128)} %bitcast.3, bf16[768,384]{1,0:T(8,128)(2,1)} %wq_hbm.1, bf16[768,384]{1,0:T(8,128)(2,1)} %wk_hbm.1, bf16[768,384]{1,0:T(8,128)(2,1)} %wv_hbm.1, bf16[384,768]{1,0:T(8,128)(2,1)} %wo_hbm.1, ...), custom_call_target="tpu_custom_call" | custom-call | tf_op jit(solution)/shard_map/pallas_call | solution.py:486
  44.2 0.7 %copy.13 = bf16[160,768]{1,0:T(8,128)(2,1)} copy(bf16[160,768]{1,0:T(8,128)(2,1)S(1)} %shard_map.109) | data formatting | bytes 491520

commit v7 on v5

--- a/solution.py
+++ b/solution.py
@@ -431,12 +431,12 @@
     hidden_left = send_left(edge_hidden.at[0:EDGE], right_hidden, left_side)
     gated = jax.nn.gelu(dot(norm_rows(hidden).astype(BF16), wu[...]), approximate=True)
     down_out[...] = dot(gated.astype(BF16), wd[...]).astype(BF16)
+    down_move = send(down_out, down_in, partner)
     ends = []
     for n, side in enumerate((mp, 1 - mp)):
         there = slice(n * EDGE, (n + 1) * EDGE)
         ends.append(send_right(down_out.at[KEPT - EDGE : KEPT], left_down.at[there], (right, side)))
         ends.append(send_left(down_out.at[0:EDGE], right_down.at[there], (left, side)))
-    down_move = send(down_out, down_in, partner)
     hidden_right.wait_recv()
     hidden_left.wait_recv()
     down_move.wait_recv()

time: 43.6 us -> 44.4 us (1.018)
  Pallas kernels: 42.9 us -> 43.6 us
    pallas_call x1, Pallas kernels: 42.9 us -> 43.6 us  [body(): pl.pallas_call(functools.partial(kernel, nx, nz), out_shape=pltpu.VMEM((r...]
where the time goes in v7:
time: 44.4 us; the launch traced here: 44.3 us
  Pallas kernels  43.6 us (98%)
  local copies, waits for them, and re-layouts  0.7 us (2%)
    pallas_call x1, Pallas kernels, body(): pl.pallas_call(functools.partial(kernel, nx, nz), out_shape=pltpu.VMEM((r...  43.6 us

profile of v7, /device:TPU:1, one launch (start us, length us, event | category | flops | bytes accessed | tf_op | source)
XLA Modules:
  0.0 44.3 jit_solution(1135333699167223178)
XLA Ops:
  0.0 43.6 %shard_map.109 = bf16[160,768]{1,0:T(8,128)(2,1)S(1)} custom-call(bf16[160,768]{1,0:T(8,128)(2,1)} %patches_hbm.1, s32[160,128]{1,0:T(8,128)} %bitcast.2, s32[160,128]{1,0:T(8,128)} %bitcast.3, bf16[768,384]{1,0:T(8,128)(2,1)} %wq_hbm.1, bf16[768,384]{1,0:T(8,128)(2,1)} %wk_hbm.1, bf16[768,384]{1,0:T(8,128)(2,1)} %wv_hbm.1, bf16[384,768]{1,0:T(8,128)(2,1)} %wo_hbm.1, ...), custom_call_target="tpu_custom_call" | custom-call | tf_op jit(solution)/shard_map/pallas_call | solution.py:477
  43.6 0.7 %copy.13 = bf16[160,768]{1,0:T(8,128)(2,1)} copy(bf16[160,768]{1,0:T(8,128)(2,1)S(1)} %shard_map.109) | data formatting | bytes 491520
